TPU v7x, 32 devices: a whole 2x2x4 slice. The times are simulated.
32 devices in a mesh: clus: 4 (over y, x), blk: 8 (over z, core).
Axes of the slice: x: 2, y: 2, z: 4, core: 2. Of those that a mesh axis runs over, the one named last changes fastest.
Arguments:
- leaf_basis: bfloat16 [256, 256, 128], P(('clus', 'blk')), may hold values from -6 to 6
- transfer: float32 [256, 128, 256], P(('clus', 'blk')), may hold values from -0.08 to 1.68
- block_rows: bfloat16 [512, 256, 192], P(('clus', 'blk')), may hold values from -6 to 6
- block_cols: bfloat16 [512, 256, 192], P(('clus', 'blk')), may hold values from -0.4375 to 0.4375
- rank_slabs: int32 [512], P(('clus', 'blk')), may hold values from 1 to 3, as said below
- row_leaf: int32 [512], P(('clus', 'blk')), may hold values from 0 to 63
- col_group: int32 [512, 1], P(('clus', 'blk')), may hold values from 0 to 3; in each aligned block of 16 rows (0 to 15, 16 to 31, ...) at most 8 rows name the same one
- col_leaf: int32 [512], P(('clus', 'blk')), may hold values from 0 to 63
Outputs:
- coupling: float32 [512, 128, 128], P(('clus', 'blk'))
- transfer_new: float32 [256, 128, 256], P(('clus', 'blk'))
Inputs may be any that keep to these rules, and one draw needn't show every extreme that they name: `col_group`: among the 16 blocks of one device at most 8 have the same column group. `rank_slabs`: some block has 3 granules and some has one.
All inputs are finite; a program needn't handle non-finite values.
Results may differ from a plain program's by a relative error of at most 0.0058.
Values may be sent and summed in bfloat16 or wider, within the bound.
No kernel may reach another device: no remote copies, remote signals or barrier semaphores. Data moves between devices by JAX's collectives and lax.ppermute only.
A program may use at most 128 MiB of HBM per device.

v0:
```python
import functools

import jax
import jax.numpy as jnp
from jax import lax
from jax.experimental import pallas as pl
from jax.experimental.pallas import tpu as pltpu
from jax.sharding import PartitionSpec as P

SLAB = 64
PANEL = 8
STRIP = 32
FIRST = 10
AHEAD = 4
VMEM_LIMIT = 24 * 1024 * 1024

NN = (((1,), (0,)), ((), ()))
NT = (((1,), (1,)), ((), ()))
TN = (((0,), (0,)), ((), ()))


def params():
    return pltpu.CompilerParams(vmem_limit_bytes=VMEM_LIMIT)


def cost(flops, moved):
    return pl.CostEstimate(flops=flops, bytes_accessed=moved, transcendentals=0)


def dot(left, right, dims):
    return lax.dot_general(left, right, dims, preferred_element_type=jnp.float32)


def split(value):
    high = value.astype(jnp.bfloat16)
    low = (value - high.astype(jnp.float32)).astype(jnp.bfloat16)
    return high, low


def dot_split(left, right, dims):
    (lh, ll), (rh, rl) = left, right
    return dot(lh, rh, dims) + (dot(lh, rl, dims) + dot(ll, rh, dims))


def lower_part(value):
    rows = lax.broadcasted_iota(jnp.int32, value.shape, 0)
    cols = lax.broadcasted_iota(jnp.int32, value.shape, 1)
    return jnp.where(cols <= rows, value, 0.0)


def factor(work, batch, size):
    lane = lax.broadcasted_iota(jnp.int32, (batch, size), 1)

    def spread(row, column):
        return jnp.broadcast_to(row[:, column : column + 1], (batch, size))

    for top in range(0, size, STRIP):
        rows = [work[pl.ds(top + i, batch, stride=size), :] for i in range(STRIP)]
        for q in range(0, STRIP, PANEL):
            first = top + q
            inside = (lane >= first) & (lane < first + PANEL)
            diag = {
                (i, j): spread(rows[q + i], first + j) for i in range(PANEL) for j in range(i, PANEL)
            }
            scale, upper = [], {}
            for k in range(PANEL):
                inv = lax.rsqrt(diag[k, k])
                scale.append(inv)
                for j in range(k + 1, PANEL):
                    upper[k, j] = diag[k, j] * inv
                for i in range(k + 1, PANEL):
                    for j in range(i, PANEL):
                        diag[i, j] = diag[i, j] - upper[k, i] * upper[k, j]
            done = []
            for k in range(PANEL):
                row = jnp.where(inside, jnp.where(lane == first + k, 1.0, 0.0), rows[q + k])
                for m in range(k):
                    row = row - upper[m, k] * done[m]
                done.append(row * scale[k])
            rows[q : q + PANEL] = done
            for i in range(q + PANEL, STRIP):
                row = jnp.where(inside, 0.0, rows[i])
                for k in range(PANEL):
                    row = row - spread(done[k], top + i) * done[k]
                rows[i] = row
        for i in range(STRIP):
            work[pl.ds(top + i, batch, stride=size), :] = rows[i]
        below = top + STRIP
        if below < size:
            for b in range(batch):
                strip = work[b * size + top : b * size + below, :]
                row = lax.broadcasted_iota(jnp.int32, strip.shape, 0) + top
                column = lax.broadcasted_iota(jnp.int32, strip.shape, 1)
                keep = (column <= row) | (column >= below)
                high, low = split(strip)
                left = jnp.concatenate([high, high, low], axis=0)
                high, low = split(jnp.where(keep, strip, 0.0))
                right = jnp.concatenate([high, low, high], axis=0)
                rest = work[b * size + below : (b + 1) * size, :]
                column = lax.broadcasted_iota(jnp.int32, rest.shape, 1)
                rest = jnp.where((column >= top) & (column < below), 0.0, rest)
                work[b * size + below : (b + 1) * size, :] = rest - dot(left, right, TN)[below:]


def leaf_kernel(leaves, group, leaf_of, basis, code, rows_out, *rest):
    pieces, work = rest[:-1], rest[-1]
    count, points, rank = basis.shape

    def pack(b, carry):
        code[b] = group[b] * leaves + leaf_of[b]
        return carry

    lax.fori_loop(0, code.shape[0], pack, 0)
    for b in range(count):
        leaf = basis[b]
        work[b * rank : (b + 1) * rank, :] = dot(leaf, leaf, TN)
    factor(work, count, rank)
    for b in range(count):
        high, low = split(lower_part(work[b * rank : (b + 1) * rank, :]))
        leaf = basis[b]
        value = (dot(leaf, high, NT) + dot(leaf, low, NT)).astype(rows_out.dtype)
        rows_out[b] = value
        for span, piece in zip(points_split(points), pieces):
            piece[b] = value[span]


def parent_top_kernel(own_basis, own_transfer, far_basis, far_transfer, weighted, top, cross, corner):
    count, points, rank = own_basis.shape
    half = own_transfer.shape[2] // 2
    for j in range(count):
        other = (j + count // 2) % count
        total = None
        for basis, transfer, c in ((own_basis, own_transfer, j), (far_basis, far_transfer, other)):
            leaf = basis[c]
            gram = split(dot(leaf, leaf, TN))
            value = transfer[c]
            moved = dot_split(gram, split(value), NN)
            if basis is own_basis:
                weighted[c] = moved
            left, right = split(value[:, :half]), split(value[:, half:])
            moved_left, moved_right = split(moved[:, :half]), split(moved[:, half:])
            parts = (
                dot_split(left, moved_left, TN),
                dot_split(right, moved_left, TN),
                dot_split(right, moved_right, TN),
            )
            total = parts if total is None else tuple(a + b for a, b in zip(total, parts))
        top[j * half : (j + 1) * half, :] = total[0]
        cross[j] = total[1]
        corner[j] = total[2]
    factor(top, count, half)


def parent_low_kernel(leaf_work, weighted, top, cross, corner, out, work, coupled):
    count, rank, columns = weighted.shape
    half = columns // 2
    for j in range(count):
        inverse = split(lower_part(top[j * half : (j + 1) * half, :]))
        lower = dot_split(split(cross[j]), inverse, NT)
        coupled[j] = lower
        lower = split(lower)
        work[j * half : (j + 1) * half, :] = corner[j] - dot_split(lower, lower, NT)
    factor(work, count, half)
    for j in range(count):
        leaf_inverse = split(lower_part(leaf_work[j * rank : (j + 1) * rank, :]))
        stacked = dot_split(leaf_inverse, split(weighted[j]), NN)
        inverse = split(lower_part(top[j * half : (j + 1) * half, :]))
        first = dot_split(split(stacked[:, :half]), inverse, NT)
        rest = stacked[:, half:] - dot_split(split(first), split(coupled[j]), NT)
        inverse = split(lower_part(work[j * half : (j + 1) * half, :]))
        out[j, :, :half] = first
        out[j, :, half:] = dot_split(split(rest), inverse, NT)


def leaf_stage(leaf_basis, leaves, group, leaf_of):
    count, points, rank = leaf_basis.shape
    smem, vmem = pl.BlockSpec(memory_space=pltpu.SMEM), pl.BlockSpec(memory_space=pltpu.VMEM)
    parts = [points] + [span.stop - span.start for span in points_split(points)]
    return pl.pallas_call(
        functools.partial(leaf_kernel, leaves),
        in_specs=[smem, smem, vmem],
        out_specs=[smem] + [vmem] * (len(parts) + 1),
        out_shape=[jax.ShapeDtypeStruct(leaf_of.shape, jnp.int32)]
        + [jax.ShapeDtypeStruct((count, part, rank), jnp.bfloat16) for part in parts]
        + [jax.ShapeDtypeStruct((count * rank, rank), jnp.float32)],
        compiler_params=params(),
        cost_estimate=cost(10**9, 25 * 10**6),
        name="leaf_factor",
    )(group, leaf_of, leaf_basis)


def parent_top(leaf_basis, transfer, far_basis, far_transfer):
    count, points, rank = leaf_basis.shape
    half = transfer.shape[2] // 2
    square = jax.ShapeDtypeStruct((count, half, half), jnp.float32)
    return pl.pallas_call(
        parent_top_kernel,
        out_shape=(
            jax.ShapeDtypeStruct(transfer.shape, jnp.float32),
            jax.ShapeDtypeStruct((count * half, half), jnp.float32),
            square,
            square,
        ),
        compiler_params=params(),
        cost_estimate=cost(10**9, 46 * 10**6),
        name="parent_top",
    )(leaf_basis, transfer, far_basis, far_transfer)


def parent_low(transfer, leaf_work, halves):
    count, rank, columns = transfer.shape
    half = columns // 2
    return pl.pallas_call(
        parent_low_kernel,
        out_shape=jax.ShapeDtypeStruct(transfer.shape, jnp.float32),
        scratch_shapes=[
            pltpu.VMEM((count * half, half), jnp.float32),
            pltpu.VMEM((count, half, half), jnp.float32),
        ],
        compiler_params=params(),
        cost_estimate=cost(10**9, 40 * 10**6),
        name="parent_low",
    )(leaf_work, *halves)


def quotient(value, size):
    return value >> (size.bit_length() - 1) if size & (size - 1) == 0 else lax.div(value, size)


def remainder(value, size):
    return value & (size - 1) if size & (size - 1) == 0 else lax.rem(value, size)


def shift(value, axis, d):
    pairs = [(index ^ d, index) for index in range(lax.axis_size(axis))]
    return lax.ppermute(value, axis, pairs)


def joined(values, bit):
    return jnp.concatenate([values, shift(values, "clus", bit)], axis=0)


def in_order(table):
    return [table[d] for d in range(len(table))]


def points_split(points):
    first = points * FIRST // 16
    return (slice(0, first), slice(first, points))


def pick(table, leaf, span, store):
    count = table[0].shape[0]
    place = quotient(leaf, count) ^ lax.axis_index("blk")
    for d in range(len(table)):

        @pl.when(place == d)
        def _():
            rows = span if table[d].shape[1] > span.stop - span.start else slice(None)
            store(table[d][remainder(leaf, count), rows, :])


def serve_kernel(size, span, asked, *refs):
    table, outs = refs[:size], refs[size:]
    me = lax.axis_index("clus")
    leaves = size * table[0].shape[0]
    for d in range(1, asked.shape[0]):

        def place(b, position, d=d):
            code = asked[d, b]
            mine = quotient(code, leaves) == me

            @pl.when(mine)
            def _():
                def store(value):
                    outs[d - 1][position] = value

                pick(table, remainder(code, leaves), span, store)

            return position + mine.astype(jnp.int32)

        lax.fori_loop(0, asked.shape[1], place, jnp.int32(0))


def serve(asked, table, span, capacity):
    groups, size = asked.shape[0], len(table)
    smem, vmem = pl.BlockSpec(memory_space=pltpu.SMEM), pl.BlockSpec(memory_space=pltpu.VMEM)
    shape = (capacity, span.stop - span.start, table[0].shape[2])
    return pl.pallas_call(
        functools.partial(serve_kernel, size, span),
        in_specs=[smem] + [vmem] * size,
        out_specs=[vmem] * (groups - 1),
        out_shape=[jax.ShapeDtypeStruct(shape, table[0].dtype)] * (groups - 1),
        compiler_params=params(),
        cost_estimate=cost(10**9, 6 * 10**6),
        name="serve",
    )(asked, *table)


def near_kernel(size, leaf, slabs, *refs):
    table, (factors, out, held) = refs[:-3], refs[-3:]
    count, width, points = factors.shape
    spans = points_split(points)

    def gather(b, carry):
        for c in range(len(spans)):

            def store(value, c=c):
                held[b, spans[c], :] = value

            pick(table[c * size : (c + 1) * size], leaf[b], spans[c], store)
        return carry

    lax.fori_loop(0, count, gather, 0)
    row = lax.broadcasted_iota(jnp.int32, (width, out.shape[1]), 0)
    for b in range(count):
        value = dot(factors[b], held[b], NN)
        value = jnp.where(row < slabs[b] * SLAB, value, 0.0)
        out[b] = value.T.astype(out.dtype)


def near_stage(row_leaf, rank_slabs, tables, factors):
    count, width, points = factors.shape
    size, rank = len(tables[0]), tables[0][0].shape[2]
    smem, vmem = pl.BlockSpec(memory_space=pltpu.SMEM), pl.BlockSpec(memory_space=pltpu.VMEM)
    flat = [piece for table in tables for piece in table]
    return pl.pallas_call(
        functools.partial(near_kernel, size),
        in_specs=[smem, smem] + [vmem] * len(flat) + [vmem],
        out_specs=vmem,
        out_shape=jax.ShapeDtypeStruct((count, rank, width), jnp.bfloat16),
        scratch_shapes=[pltpu.VMEM((count, points, rank), flat[0].dtype)],
        compiler_params=params(),
        cost_estimate=cost(10**9, 10 * 10**6),
        name="near",
    )(row_leaf, rank_slabs, *flat, factors)


def far_kernel(groups, size, chunks, code, slabs, near, *refs):
    table, refs = refs[: chunks * size], refs[chunks * size :]
    fetched, (factors, out, held, tally) = refs[: chunks * (groups - 1)], refs[chunks * (groups - 1) :]
    count, width, points = factors.shape
    leaves = size * table[0].shape[0]
    spans = points_split(points)
    me = lax.axis_index("clus")
    for g in range(groups):
        tally[g] = 0

    def gather(b, carry):
        group, leaf = quotient(code[b], leaves), remainder(code[b], leaves)
        position = tally[group]
        tally[group] = position + 1
        away = group ^ me

        @pl.when(away == 0)
        def _():
            for c in range(chunks):

                def store(value, c=c):
                    held[b, spans[c], :] = value

                pick(table[c * size : (c + 1) * size], leaf, spans[c], store)

        for d in range(1, groups):

            @pl.when(away == d)
            def _(d=d):
                for c in range(chunks):
                    piece = fetched[c * (groups - 1) + d - 1]
                    held[b, spans[c], :] = piece[position]

        return carry

    lax.fori_loop(0, count, gather, 0)
    row = lax.broadcasted_iota(jnp.int32, (width, near.shape[1]), 0)
    for first in range(0, count, AHEAD):
        values = [dot(factors[b], held[b], NN) for b in range(first, first + AHEAD)]
        for b in range(first, first + AHEAD):
            value = jnp.where(row < slabs[b] * SLAB, values[b - first], 0.0).astype(near.dtype)
            out[b] = dot(near[b], value, NN)


def far_stage(code, rank_slabs, near, tables, fetched, factors):
    count, width, points = factors.shape
    size, rank = len(tables[0]), tables[0][0].shape[2]
    groups = len(fetched[0]) + 1
    smem, vmem = pl.BlockSpec(memory_space=pltpu.SMEM), pl.BlockSpec(memory_space=pltpu.VMEM)
    flat = [piece for table in tables for piece in table] + [piece for part in fetched for piece in part]
    return pl.pallas_call(
        functools.partial(far_kernel, groups, size, len(tables)),
        in_specs=[smem, smem, vmem] + [vmem] * len(flat) + [vmem],
        out_specs=vmem,
        out_shape=jax.ShapeDtypeStruct((count, rank, rank), jnp.float32),
        scratch_shapes=[
            pltpu.VMEM((count, points, rank), flat[0].dtype),
            pltpu.SMEM((groups,), jnp.int32),
        ],
        compiler_params=params(),
        cost_estimate=cost(10**9, 13 * 10**6),
        name="far",
    )(code, rank_slabs, near, *flat, factors)


def per_device(
    leaf_basis, transfer, block_rows, block_cols, rank_slabs, row_leaf, col_group, col_leaf
):
    groups, size = lax.axis_size("clus"), lax.axis_size("blk")
    capacity = max(2, 2 * block_rows.shape[0] // groups)
    spans = points_split(leaf_basis.shape[1])
    barrier = lax.optimization_barrier
    far_basis = shift(leaf_basis, "blk", 1)
    far_transfer = shift(transfer, "blk", 1)
    code, rows, first, second, leaf_work = leaf_stage(
        leaf_basis, leaf_basis.shape[0] * size, col_group[:, 0], col_leaf
    )
    code, rows, first, second, far_basis, far_transfer = barrier(
        (code, rows, first, second, far_basis, far_transfer)
    )
    chips = range(4, size, 2)
    table = {d: shift(first, "blk", d) for d in reversed(chips)}
    close = {0: rows, 1: shift(rows, "blk", 1), 2: shift(rows, "blk", 2)}
    asked = joined(code[None], 1)
    halves = parent_top(leaf_basis, transfer, far_basis, far_transfer)
    asked, close[1], second, halves = barrier((asked, close[1], second, halves))
    later = {d: shift(second, "blk", d) for d in reversed(chips)}
    bit = 2
    while bit < groups:
        asked = joined(asked, bit)
        bit *= 2
    transfer_new = parent_low(transfer, leaf_work, halves)
    table, close, asked, transfer_new = barrier((table, close, asked, transfer_new))
    for d in chips:
        table[d + 1] = shift(table[d], "blk", 1)
    close[3] = shift(close[2], "blk", 1)
    served = serve(asked, in_order(close | table), spans[0], capacity)
    fetched = [[shift(value, "clus", d + 1) for d, value in enumerate(served)]]
    for d in chips:
        later[d + 1] = shift(later[d], "blk", 1)
    later, fetched[0] = barrier((later, fetched[0]))
    served = serve(asked, in_order(close | later), spans[1], capacity)
    fetched.append([shift(value, "clus", d + 1) for d, value in enumerate(served)])
    tables = [in_order(close | table), in_order(close | later)]
    near = near_stage(row_leaf, rank_slabs, tables, jnp.swapaxes(block_rows, 1, 2))
    coupling = far_stage(asked[0], rank_slabs, near, tables, fetched, jnp.swapaxes(block_cols, 1, 2))
    return (coupling, transfer_new)


def solution(mesh):
    placed = (
        P(("clus", "blk"), None, None),
        P(("clus", "blk"), None, None),
        P(("clus", "blk"), None, None),
        P(("clus", "blk"), None, None),
        P(("clus", "blk")),
        P(("clus", "blk")),
        P(("clus", "blk"), None),
        P(("clus", "blk")),
    )
    return jax.shard_map(
        per_device,
        mesh=mesh,
        in_specs=placed,
        out_specs=(P(("clus", "blk"), None, None), P(("clus", "blk"), None, None)),
        check_vma=False,
    )
```

profile of v0, /device:TPU:0, one launch (start us, length us, event | category | flops | bytes accessed | tf_op | source)
XLA Modules:
  0.0 85.7 jit_solution(5072954699518126273)
XLA Ops:
  0.6 0.5 collective-permute-start.1
  1.1 0.1 collective-permute-start
  1.2 1.0 %copy-done.5 = bf16[8,256,128]{2,1,0:T(8,128)(2,1)S(1)} copy-done((bf16[8,256,128]{2,1,0:T(8,128)(2,1)S(1)}, bf16[8,256,128]{2,1,0:T(8,128)(2,1)}, u32[]{:S(2)}) %copy-start.5) | copy-done | bytes 524312
  2.3 0.7 copy-done.6
  2.9 0.7 copy-done.7
  3.6 7.0 %leaf_factor.1 = (s32[16]{0:T(128)S(1)}, bf16[8,256,128]{2,1,0:T(8,128)(2,1)S(1)}, bf16[8,160,128]{2,1,0:T(8,128)(2,1)S(1)}, bf16[8,96,128]{2,1,0:T(8,128)(2,1)S(1)}, f32[1024,128]{1,0:T(8,128)S(1)}) custom-call(s32[16]{0:T(128)S(1)} %bitcast.10, s32[16]{0:T(128)S(1)} %copy-done.7, bf16[8,256,128]{2,1,0:T(8,128)(2,1)S(1)} %copy-done.5), custom_call_target="tpu_custom_call" | custom-call | flops 1000000000 | bytes 25000000 | tf_op jit(solution)/shard_map/leaf_factor/pallas_call | solution.py:179
  10.6 0.0 collective-permute-done.1.far_transfer
  10.6 0.5 collective-permute-start.5
  11.1 2.6 %collective-permute-start.6 = (bf16[8,256,128]{2,1,0:T(8,128)(2,1)S(1)}, bf16[8,256,128]{2,1,0:T(8,128)(2,1)S(1)}, u32[]{:S(2)}, u32[]{:S(2)}) collective-permute-start(bf16[8,256,128]{2,1,0:T(8,128)(2,1)S(1)} %get-tuple-element.66.refs_0_.refs_8_), channel_id=1, source_target_pairs={{2,0},{3,1},{0,2},{1,3},{6,4},{7,5},{4,6},{5,7},{10,8},{11,9},{8,1... | collective-permute-start | bytes 1572872 | tf_op jit(solution)/shard_map/ppermute | solution.py:236
  13.8 2.5 %collective-permute-start.3 = (bf16[8,160,128]{2,1,0:T(8,128)(2,1)S(1)}, bf16[8,160,128]{2,1,0:T(8,128)(2,1)S(1)}, u32[]{:S(2)}, u32[]{:S(2)}) collective-permute-start(bf16[8,160,128]{2,1,0:T(8,128)(2,1)S(1)} %get-tuple-element.48), channel_id=1, source_target_pairs={{6,0},{7,1},{4,2},{5,3},{2,4},{3,5},{0,6},{1,7},{14,8},{15,9},{12,... | collective-permute-start | bytes 983048 | tf_op jit(solution)/shard_map/ppermute | solution.py:236
  16.2 0.1 collective-permute-start.2
  16.4 1.5 %collective-permute-start.4 = (s32[1,16]{1,0:T(1,128)S(1)}, s32[1,16]{1,0:T(1,128)S(1)}, u32[]{:S(2)}, u32[]{:S(2)}) collective-permute-start(s32[1,16]{1,0:T(1,128)S(1)} %bitcast.8), channel_id=1, source_target_pairs={{8,0},{0,8},{24,16},{16,24},{9,1},{1,9},{25,17},{17,25},{10,2},{2,... | collective-permute-start | bytes 200 | tf_op jit(solution)/shard_map/ppermute | solution.py:236
  17.8 12.6 %parent_top.1 = (f32[8,128,256]{2,1,0:T(8,128)S(1)}, f32[1024,128]{1,0:T(8,128)S(1)}, f32[8,128,128]{2,1,0:T(8,128)S(1)}, f32[8,128,128]{2,1,0:T(8,128)S(1)}) custom-call(bf16[8,256,128]{2,1,0:T(8,128)(2,1)S(1)} %copy-done.5, f32[8,128,256]{2,1,0:T(8,128)S(1)} %copy-done.4, bf16[8,256,128]{2,1,0:T(8,128)(2,1)S(1)} %collective-permute-done.far_basis, ...), custom_call_target="tpu_custom_call" | custom-call | flops 1000000000 | bytes 46000000 | tf_op jit(solution)/shard_map/parent_top/pallas_call | solution.py:196
  30.5 0.0 collective-permute-done.4
  30.5 0.0 collective-permute-done.5.refs_1_.refs_9_
  30.5 1.6 %collective-permute-start.7 = (s32[2,16]{1,0:T(2,128)S(1)}, s32[2,16]{1,0:T(2,128)S(1)}, u32[]{:S(2)}, u32[]{:S(2)}) collective-permute-start(s32[2,16]{1,0:T(2,128)S(1)} %pad_add_fusion.1), channel_id=1, source_target_pairs={{16,0},{24,8},{0,16},{8,24},{17,1},{25,9},{1,17},{9,25},{18,2},{26... | collective-permute-start | bytes 392 | tf_op jit(solution)/shard_map/ppermute | solution.py:236
  32.1 11.1 %parent_low.1 = f32[8,128,256]{2,1,0:T(8,128)} custom-call(f32[1024,128]{1,0:T(8,128)S(1)} %get-tuple-element.60.leaf_work, f32[8,128,256]{2,1,0:T(8,128)S(1)} %get-tuple-element.61.weighted, f32[1024,128]{1,0:T(8,128)S(1)} %get-tuple-element.62.top, f32[8,128,128]{2,1,0:T(8,128)S(1)} %get-tuple-element.63.cross, f32[8,128,128]{2,1,0:T(8,128)S(1)} %get-tuple-element.64.corner), custom_call_target="tpu_custom_call" | custom-call | flops 1000000000 | bytes 40000000 | tf_op jit(solution)/shard_map/parent_low/pallas_call | solution.py:213
  43.2 0.0 collective-permute-done.7
  43.2 0.0 collective-permute-done.3.refs_6_
  43.2 2.3 %collective-permute-done.2.refs_4_ = bf16[8,160,128]{2,1,0:T(8,128)(2,1)S(1)} collective-permute-done((bf16[8,160,128]{2,1,0:T(8,128)(2,1)S(1)}, bf16[8,160,128]{2,1,0:T(8,128)(2,1)S(1)}, u32[]{:S(2)}, u32[]{:S(2)}) %collective-permute-start.2) | collective-permute-done | bytes 327712 | tf_op jit(solution)/shard_map/ppermute | solution.py:236
  45.5 0.0 collective-permute-done.6.refs_2_.refs_10_
  45.5 0.0 collective-permute-start.8
  45.5 0.5 collective-permute-start.9
  46.0 0.0 collective-permute-start.10
  46.0 2.6 %collective-permute-start.13 = (bf16[8,96,128]{2,1,0:T(8,128)(2,1)S(1)}, bf16[8,96,128]{2,1,0:T(8,128)(2,1)S(1)}, u32[]{:S(2)}, u32[]{:S(2)}) collective-permute-start(bf16[8,96,128]{2,1,0:T(8,128)(2,1)S(1)} %get-tuple-element.71), channel_id=1, source_target_pairs={{6,0},{7,1},{4,2},{5,3},{2,4},{3,5},{0,6},{1,7},{14,8},{15,9},{12,... | collective-permute-start | bytes 589832 | tf_op jit(solution)/shard_map/ppermute | solution.py:236
  48.7 0.0 collective-permute-start.11
  48.7 0.0 collective-permute-done.9.refs_5_
  48.7 0.0 collective-permute-done.10.refs_7_
  48.7 0.0 collective-permute-done.8.refs_3_.refs_11_
  48.7 2.3 %serve.2 = (bf16[8,160,128]{2,1,0:T(8,128)(2,1)S(1)}, bf16[8,160,128]{2,1,0:T(8,128)(2,1)S(1)}, bf16[8,160,128]{2,1,0:T(8,128)(2,1)S(1)}) custom-call(s32[4,16]{1,0:T(4,128)S(1)} %pad_add_fusion.asked, bf16[8,256,128]{2,1,0:T(8,128)(2,1)S(1)} %get-tuple-element.66.refs_0_.refs_8_, bf16[8,256,128]{2,1,0:T(8,128)(2,1)S(1)} %collective-permute-done.5.refs_1_.refs_9_, ...), custom_call_target="tpu_custom_call" | custom-call | flops 1000000000 | bytes 6000000 | tf_op jit(solution)/shard_map/serve/pallas_call | solution.py:289
  51.0 1.0 %collective-permute-start.15 = (bf16[8,160,128]{2,1,0:T(8,128)(2,1)S(1)}, bf16[8,160,128]{2,1,0:T(8,128)(2,1)S(1)}, u32[]{:S(2)}, u32[]{:S(2)}) collective-permute-start(bf16[8,160,128]{2,1,0:T(8,128)(2,1)S(1)} %get-tuple-element.72), channel_id=1, source_target_pairs={{8,0},{0,8},{24,16},{16,24},{9,1},{1,9},{25,17},{17,25},{10,2},{2,... | collective-permute-start | bytes 983048 | tf_op jit(solution)/shard_map/ppermute | solution.py:236
  52.0 1.4 %collective-permute-start.16 = (bf16[8,160,128]{2,1,0:T(8,128)(2,1)S(1)}, bf16[8,160,128]{2,1,0:T(8,128)(2,1)S(1)}, u32[]{:S(2)}, u32[]{:S(2)}) collective-permute-start(bf16[8,160,128]{2,1,0:T(8,128)(2,1)S(1)} %get-tuple-element.73), channel_id=1, source_target_pairs={{16,0},{24,8},{0,16},{8,24},{17,1},{25,9},{1,17},{9,25},{18,2},{26... | collective-permute-start | bytes 983048 | tf_op jit(solution)/shard_map/ppermute | solution.py:236
  53.4 1.1 %collective-permute-start.17 = (bf16[8,160,128]{2,1,0:T(8,128)(2,1)S(1)}, bf16[8,160,128]{2,1,0:T(8,128)(2,1)S(1)}, u32[]{:S(2)}, u32[]{:S(2)}) collective-permute-start(bf16[8,160,128]{2,1,0:T(8,128)(2,1)S(1)} %get-tuple-element.74), channel_id=1, source_target_pairs={{24,0},{16,8},{8,16},{0,24},{25,1},{17,9},{9,17},{1,25},{26,2},{18... | collective-permute-start | bytes 983048 | tf_op jit(solution)/shard_map/ppermute | solution.py:236
  54.5 1.1 %collective-permute-done.13.refs_14_.refs_6_ = bf16[8,96,128]{2,1,0:T(8,128)(2,1)S(1)} collective-permute-done((bf16[8,96,128]{2,1,0:T(8,128)(2,1)S(1)}, bf16[8,96,128]{2,1,0:T(8,128)(2,1)S(1)}, u32[]{:S(2)}, u32[]{:S(2)}) %collective-permute-start.13) | collective-permute-done | bytes 196640 | tf_op jit(solution)/shard_map/ppermute | solution.py:236
  55.6 9.6 %collective-permute-done.11.refs_12_.refs_4_ = bf16[8,96,128]{2,1,0:T(8,128)(2,1)S(1)} collective-permute-done((bf16[8,96,128]{2,1,0:T(8,128)(2,1)S(1)}, bf16[8,96,128]{2,1,0:T(8,128)(2,1)S(1)}, u32[]{:S(2)}, u32[]{:S(2)}) %collective-permute-start.11) | collective-permute-done | bytes 196640 | tf_op jit(solution)/shard_map/ppermute | solution.py:236
  65.2 1.4 %collective-permute-done.12.refs_13_.refs_5_ = bf16[8,96,128]{2,1,0:T(8,128)(2,1)S(1)} collective-permute-done((bf16[8,96,128]{2,1,0:T(8,128)(2,1)S(1)}, bf16[8,96,128]{2,1,0:T(8,128)(2,1)S(1)}, u32[]{:S(2)}, u32[]{:S(2)}) %collective-permute-start.12) | collective-permute-done | bytes 196640 | tf_op jit(solution)/shard_map/ppermute | solution.py:236
  66.7 0.0 collective-permute-done.15.refs_16_
  66.7 1.9 %collective-permute-done.16.refs_17_ = bf16[8,160,128]{2,1,0:T(8,128)(2,1)S(1)} collective-permute-done((bf16[8,160,128]{2,1,0:T(8,128)(2,1)S(1)}, bf16[8,160,128]{2,1,0:T(8,128)(2,1)S(1)}, u32[]{:S(2)}, u32[]{:S(2)}) %collective-permute-start.16) | collective-permute-done | bytes 327712 | tf_op jit(solution)/shard_map/ppermute | solution.py:236
  68.6 2.3 %serve.3 = (bf16[8,96,128]{2,1,0:T(8,128)(2,1)S(1)}, bf16[8,96,128]{2,1,0:T(8,128)(2,1)S(1)}, bf16[8,96,128]{2,1,0:T(8,128)(2,1)S(1)}) custom-call(s32[4,16]{1,0:T(4,128)S(1)} %pad_add_fusion.asked, bf16[8,256,128]{2,1,0:T(8,128)(2,1)S(1)} %get-tuple-element.66.refs_0_.refs_8_, bf16[8,256,128]{2,1,0:T(8,128)(2,1)S(1)} %collective-permute-done.5.refs_1_.refs_9_, ...), custom_call_target="tpu_custom_call" | custom-call | flops 1000000000 | bytes 6000000 | tf_op jit(solution)/shard_map/serve/pallas_call | solution.py:289
  70.8 0.7 collective-permute-start.18
  71.6 0.9 %collective-permute-start.19 = (bf16[8,96,128]{2,1,0:T(8,128)(2,1)S(1)}, bf16[8,96,128]{2,1,0:T(8,128)(2,1)S(1)}, u32[]{:S(2)}, u32[]{:S(2)}) collective-permute-start(bf16[8,96,128]{2,1,0:T(8,128)(2,1)S(1)} %get-tuple-element.83), channel_id=1, source_target_pairs={{16,0},{24,8},{0,16},{8,24},{17,1},{25,9},{1,17},{9,25},{18,2},{26... | collective-permute-start | bytes 589832 | tf_op jit(solution)/shard_map/ppermute | solution.py:236
  72.5 1.9 %collective-permute-start.20 = (bf16[8,96,128]{2,1,0:T(8,128)(2,1)S(1)}, bf16[8,96,128]{2,1,0:T(8,128)(2,1)S(1)}, u32[]{:S(2)}, u32[]{:S(2)}) collective-permute-start(bf16[8,96,128]{2,1,0:T(8,128)(2,1)S(1)} %get-tuple-element.84), channel_id=1, source_target_pairs={{24,0},{16,8},{8,16},{0,24},{25,1},{17,9},{9,17},{1,25},{26,2},{18... | collective-permute-start | bytes 589832 | tf_op jit(solution)/shard_map/ppermute | solution.py:236
  74.4 0.0 copy-start.1
  74.4 2.9 %near.1 = bf16[16,128,192]{2,1,0:T(8,128)(2,1)S(1)} custom-call(s32[16]{0:T(128)S(1)} %copy-done.3, s32[16]{0:T(128)S(1)} %copy-done.2, bf16[8,256,128]{2,1,0:T(8,128)(2,1)S(1)} %get-tuple-element.66.refs_0_.refs_8_, bf16[8,256,128]{2,1,0:T(8,128)(2,1)S(1)} %collective-permute-done.5.refs_1_.refs_9_, ...), custom_call_target="tpu_custom_call" | custom-call | flops 1000000000 | bytes 10000000 | tf_op jit(solution)/shard_map/near/pallas_call | solution.py:327
  77.3 1.4 %collective-permute-done.18.refs_19_ = bf16[8,96,128]{2,1,0:T(8,128)(2,1)S(1)} collective-permute-done((bf16[8,96,128]{2,1,0:T(8,128)(2,1)S(1)}, bf16[8,96,128]{2,1,0:T(8,128)(2,1)S(1)}, u32[]{:S(2)}, u32[]{:S(2)}) %collective-permute-start.18) | collective-permute-done | bytes 196640 | tf_op jit(solution)/shard_map/ppermute | solution.py:236
  78.7 3.0 %collective-permute-done.19.refs_20_ = bf16[8,96,128]{2,1,0:T(8,128)(2,1)S(1)} collective-permute-done((bf16[8,96,128]{2,1,0:T(8,128)(2,1)S(1)}, bf16[8,96,128]{2,1,0:T(8,128)(2,1)S(1)}, u32[]{:S(2)}, u32[]{:S(2)}) %collective-permute-start.19) | collective-permute-done | bytes 196640 | tf_op jit(solution)/shard_map/ppermute | solution.py:236
  81.8 0.0 collective-permute-done.20.refs_21_
  81.8 3.9 %far.1 = f32[16,128,128]{2,1,0:T(8,128)} custom-call(s32[16]{0:T(128)S(1)} %slice_bitcast_fusion.code, s32[16]{0:T(128)S(1)} %copy-done.2, bf16[16,128,192]{2,1,0:T(8,128)(2,1)S(1)} %near.1, bf16[8,256,128]{2,1,0:T(8,128)(2,1)S(1)} %get-tuple-element.66.refs_0_.refs_8_, bf16[8,256,128]{2,1,0:T(8,128)(2,1)S(1)} %collective-permute-done.5.refs_1_.refs_9_, ...), custom_call_target="tpu_custom_call" | custom-call | flops 1000000000 | bytes 13000000 | tf_op jit(solution)/shard_map/far/pallas_call | solution.py:389
  (20 shorter events, 0.1 us)
Async XLA Ops:
  0.6 10.0 %collective-permute-start.1 = (f32[8,128,256]{2,1,0:T(8,128)}, f32[8,128,256]{2,1,0:T(8,128)S(1)}, u32[]{:S(2)}, u32[]{:S(2)}) collective-permute-start(f32[8,128,256]{2,1,0:T(8,128)} %own_transfer.1), channel_id=1, source_target_pairs={{1,0},{0,1},{3,2},{2,3},{5,4},{4,5},{7,6},{6,7},{9,8},{8,9},{11,10... | collective-permute-start | bytes 3145736 | tf_op jit(solution)/shard_map/ppermute | solution.py:236
  1.1 9.4 %collective-permute-start = (bf16[8,256,128]{2,1,0:T(8,128)(2,1)}, bf16[8,256,128]{2,1,0:T(8,128)(2,1)S(1)}, u32[]{:S(2)}, u32[]{:S(2)}) collective-permute-start(bf16[8,256,128]{2,1,0:T(8,128)(2,1)} %own_basis.1), channel_id=1, source_target_pairs={{1,0},{0,1},{3,2},{2,3},{5,4},{4,5},{7,6},{6,7},{9,8},{8,9},{11,10... | collective-permute-start | bytes 1572872 | tf_op jit(solution)/shard_map/ppermute | solution.py:236
  1.2 1.0 %copy-start.5 = (bf16[8,256,128]{2,1,0:T(8,128)(2,1)S(1)}, bf16[8,256,128]{2,1,0:T(8,128)(2,1)}, u32[]{:S(2)}) copy-start(bf16[8,256,128]{2,1,0:T(8,128)(2,1)} %own_basis.1) | copy-start | bytes 1572868
  2.3 0.7 copy-start.6
  2.9 0.7 copy-start.7
  3.6 14.3 %copy-start.4 = (f32[8,128,256]{2,1,0:T(8,128)S(1)}, f32[8,128,256]{2,1,0:T(8,128)}, u32[]{:S(2)}) copy-start(f32[8,128,256]{2,1,0:T(8,128)} %own_transfer.1) | copy-start | bytes 3145732
  10.6 19.9 %collective-permute-start.5 = (bf16[8,256,128]{2,1,0:T(8,128)(2,1)S(1)}, bf16[8,256,128]{2,1,0:T(8,128)(2,1)S(1)}, u32[]{:S(2)}, u32[]{:S(2)}) collective-permute-start(bf16[8,256,128]{2,1,0:T(8,128)(2,1)S(1)} %get-tuple-element.66.refs_0_.refs_8_), channel_id=1, source_target_pairs={{1,0},{0,1},{3,2},{2,3},{5,4},{4,5},{7,6},{6,7},{9,8},{8,9},{11,10... | collective-permute-start | bytes 1572872 | tf_op jit(solution)/shard_map/ppermute | solution.py:236
  11.1 34.4 %collective-permute-start.6 = (bf16[8,256,128]{2,1,0:T(8,128)(2,1)S(1)}, bf16[8,256,128]{2,1,0:T(8,128)(2,1)S(1)}, u32[]{:S(2)}, u32[]{:S(2)}) collective-permute-start(bf16[8,256,128]{2,1,0:T(8,128)(2,1)S(1)} %get-tuple-element.66.refs_0_.refs_8_), channel_id=1, source_target_pairs={{2,0},{3,1},{0,2},{1,3},{6,4},{7,5},{4,6},{5,7},{10,8},{11,9},{8,1... | collective-permute-start | bytes 1572872 | tf_op jit(solution)/shard_map/ppermute | solution.py:236
  13.8 29.5 %collective-permute-start.3 = (bf16[8,160,128]{2,1,0:T(8,128)(2,1)S(1)}, bf16[8,160,128]{2,1,0:T(8,128)(2,1)S(1)}, u32[]{:S(2)}, u32[]{:S(2)}) collective-permute-start(bf16[8,160,128]{2,1,0:T(8,128)(2,1)S(1)} %get-tuple-element.48), channel_id=1, source_target_pairs={{6,0},{7,1},{4,2},{5,3},{2,4},{3,5},{0,6},{1,7},{14,8},{15,9},{12,... | collective-permute-start | bytes 983048 | tf_op jit(solution)/shard_map/ppermute | solution.py:236
  16.2 29.3 %collective-permute-start.2 = (bf16[8,160,128]{2,1,0:T(8,128)(2,1)S(1)}, bf16[8,160,128]{2,1,0:T(8,128)(2,1)S(1)}, u32[]{:S(2)}, u32[]{:S(2)}) collective-permute-start(bf16[8,160,128]{2,1,0:T(8,128)(2,1)S(1)} %get-tuple-element.48), channel_id=1, source_target_pairs={{4,0},{5,1},{6,2},{7,3},{0,4},{1,5},{2,6},{3,7},{12,8},{13,9},{14,... | collective-permute-start | bytes 983048 | tf_op jit(solution)/shard_map/ppermute | solution.py:236
  16.4 14.1 %collective-permute-start.4 = (s32[1,16]{1,0:T(1,128)S(1)}, s32[1,16]{1,0:T(1,128)S(1)}, u32[]{:S(2)}, u32[]{:S(2)}) collective-permute-start(s32[1,16]{1,0:T(1,128)S(1)} %bitcast.8), channel_id=1, source_target_pairs={{8,0},{0,8},{24,16},{16,24},{9,1},{1,9},{25,17},{17,25},{10,2},{2,... | collective-permute-start | bytes 200 | tf_op jit(solution)/shard_map/ppermute | solution.py:236
  30.5 12.7 %collective-permute-start.7 = (s32[2,16]{1,0:T(2,128)S(1)}, s32[2,16]{1,0:T(2,128)S(1)}, u32[]{:S(2)}, u32[]{:S(2)}) collective-permute-start(s32[2,16]{1,0:T(2,128)S(1)} %pad_add_fusion.1), channel_id=1, source_target_pairs={{16,0},{24,8},{0,16},{8,24},{17,1},{25,9},{1,17},{9,25},{18,2},{26... | collective-permute-start | bytes 392 | tf_op jit(solution)/shard_map/ppermute | solution.py:236
  45.5 3.2 %collective-permute-start.8 = (bf16[8,256,128]{2,1,0:T(8,128)(2,1)S(1)}, bf16[8,256,128]{2,1,0:T(8,128)(2,1)S(1)}, u32[]{:S(2)}, u32[]{:S(2)}) collective-permute-start(bf16[8,256,128]{2,1,0:T(8,128)(2,1)S(1)} %collective-permute-done.6.refs_2_.refs_10_), channel_id=1, source_target_pairs={{1,0},{0,1},{3,2},{2,3},{5,4},{4,5},{7,6},{6,7},{9,8},{8,9},{11,10... | collective-permute-start | bytes 1572872 | tf_op jit(solution)/shard_map/ppermute | solution.py:236
  45.5 3.2 %collective-permute-start.9 = (bf16[8,160,128]{2,1,0:T(8,128)(2,1)S(1)}, bf16[8,160,128]{2,1,0:T(8,128)(2,1)S(1)}, u32[]{:S(2)}, u32[]{:S(2)}) collective-permute-start(bf16[8,160,128]{2,1,0:T(8,128)(2,1)S(1)} %collective-permute-done.2.refs_4_), channel_id=1, source_target_pairs={{1,0},{0,1},{3,2},{2,3},{5,4},{4,5},{7,6},{6,7},{9,8},{8,9},{11,10... | collective-permute-start | bytes 983048 | tf_op jit(solution)/shard_map/ppermute | solution.py:236
  46.0 2.7 %collective-permute-start.10 = (bf16[8,160,128]{2,1,0:T(8,128)(2,1)S(1)}, bf16[8,160,128]{2,1,0:T(8,128)(2,1)S(1)}, u32[]{:S(2)}, u32[]{:S(2)}) collective-permute-start(bf16[8,160,128]{2,1,0:T(8,128)(2,1)S(1)} %collective-permute-done.3.refs_6_), channel_id=1, source_target_pairs={{1,0},{0,1},{3,2},{2,3},{5,4},{4,5},{7,6},{6,7},{9,8},{8,9},{11,10... | collective-permute-start | bytes 983048 | tf_op jit(solution)/shard_map/ppermute | solution.py:236
  46.0 9.6 %collective-permute-start.13 = (bf16[8,96,128]{2,1,0:T(8,128)(2,1)S(1)}, bf16[8,96,128]{2,1,0:T(8,128)(2,1)S(1)}, u32[]{:S(2)}, u32[]{:S(2)}) collective-permute-start(bf16[8,96,128]{2,1,0:T(8,128)(2,1)S(1)} %get-tuple-element.71), channel_id=1, source_target_pairs={{6,0},{7,1},{4,2},{5,3},{2,4},{3,5},{0,6},{1,7},{14,8},{15,9},{12,... | collective-permute-start | bytes 589832 | tf_op jit(solution)/shard_map/ppermute | solution.py:236
  48.7 16.6 %collective-permute-start.11 = (bf16[8,96,128]{2,1,0:T(8,128)(2,1)S(1)}, bf16[8,96,128]{2,1,0:T(8,128)(2,1)S(1)}, u32[]{:S(2)}, u32[]{:S(2)}) collective-permute-start(bf16[8,96,128]{2,1,0:T(8,128)(2,1)S(1)} %get-tuple-element.71), channel_id=1, source_target_pairs={{4,0},{5,1},{6,2},{7,3},{0,4},{1,5},{2,6},{3,7},{12,8},{13,9},{14,... | collective-permute-start | bytes 589832 | tf_op jit(solution)/shard_map/ppermute | solution.py:236
  51.0 15.7 %collective-permute-start.15 = (bf16[8,160,128]{2,1,0:T(8,128)(2,1)S(1)}, bf16[8,160,128]{2,1,0:T(8,128)(2,1)S(1)}, u32[]{:S(2)}, u32[]{:S(2)}) collective-permute-start(bf16[8,160,128]{2,1,0:T(8,128)(2,1)S(1)} %get-tuple-element.72), channel_id=1, source_target_pairs={{8,0},{0,8},{24,16},{16,24},{9,1},{1,9},{25,17},{17,25},{10,2},{2,... | collective-permute-start | bytes 983048 | tf_op jit(solution)/shard_map/ppermute | solution.py:236
  52.0 16.6 %collective-permute-start.16 = (bf16[8,160,128]{2,1,0:T(8,128)(2,1)S(1)}, bf16[8,160,128]{2,1,0:T(8,128)(2,1)S(1)}, u32[]{:S(2)}, u32[]{:S(2)}) collective-permute-start(bf16[8,160,128]{2,1,0:T(8,128)(2,1)S(1)} %get-tuple-element.73), channel_id=1, source_target_pairs={{16,0},{24,8},{0,16},{8,24},{17,1},{25,9},{1,17},{9,25},{18,2},{26... | collective-permute-start | bytes 983048 | tf_op jit(solution)/shard_map/ppermute | solution.py:236
  53.4 21.0 %copy-start = (bf16[16,256,192]{1,2,0:T(8,128)(2,1)S(1)}, bf16[16,256,192]{1,2,0:T(8,128)(2,1)}, u32[]{:S(2)}) copy-start(bf16[16,256,192]{1,2,0:T(8,128)(2,1)} %param.10) | copy-start | bytes 4718596
  53.4 21.0 %copy-start.2 = (s32[16]{0:T(128)S(1)}, s32[16]{0:T(128)}, u32[]{:S(2)}) copy-start(s32[16]{0:T(128)} %slabs.3) | copy-start | bytes 196
  53.4 21.0 %copy-start.3 = (s32[16]{0:T(128)S(1)}, s32[16]{0:T(128)}, u32[]{:S(2)}) copy-start(s32[16]{0:T(128)} %leaf.1) | copy-start | bytes 196
  53.4 15.1 %collective-permute-start.17 = (bf16[8,160,128]{2,1,0:T(8,128)(2,1)S(1)}, bf16[8,160,128]{2,1,0:T(8,128)(2,1)S(1)}, u32[]{:S(2)}, u32[]{:S(2)}) collective-permute-start(bf16[8,160,128]{2,1,0:T(8,128)(2,1)S(1)} %get-tuple-element.74), channel_id=1, source_target_pairs={{24,0},{16,8},{8,16},{0,24},{25,1},{17,9},{9,17},{1,25},{26,2},{18... | collective-permute-start | bytes 983048 | tf_op jit(solution)/shard_map/ppermute | solution.py:236
  55.6 9.6 %collective-permute-start.14 = (bf16[8,96,128]{2,1,0:T(8,128)(2,1)S(1)}, bf16[8,96,128]{2,1,0:T(8,128)(2,1)S(1)}, u32[]{:S(2)}, u32[]{:S(2)}) collective-permute-start(bf16[8,96,128]{2,1,0:T(8,128)(2,1)S(1)} %collective-permute-done.13.refs_14_.refs_6_), channel_id=1, source_target_pairs={{1,0},{0,1},{3,2},{2,3},{5,4},{4,5},{7,6},{6,7},{9,8},{8,9},{11,10... | collective-permute-start | bytes 589832 | tf_op jit(solution)/shard_map/ppermute | solution.py:236
  65.2 1.4 %collective-permute-start.12 = (bf16[8,96,128]{2,1,0:T(8,128)(2,1)S(1)}, bf16[8,96,128]{2,1,0:T(8,128)(2,1)S(1)}, u32[]{:S(2)}, u32[]{:S(2)}) collective-permute-start(bf16[8,96,128]{2,1,0:T(8,128)(2,1)S(1)} %collective-permute-done.11.refs_12_.refs_4_), channel_id=1, source_target_pairs={{1,0},{0,1},{3,2},{2,3},{5,4},{4,5},{7,6},{6,7},{9,8},{8,9},{11,10... | collective-permute-start | bytes 589832 | tf_op jit(solution)/shard_map/ppermute | solution.py:236
  70.8 7.9 %collective-permute-start.18 = (bf16[8,96,128]{2,1,0:T(8,128)(2,1)S(1)}, bf16[8,96,128]{2,1,0:T(8,128)(2,1)S(1)}, u32[]{:S(2)}, u32[]{:S(2)}) collective-permute-start(bf16[8,96,128]{2,1,0:T(8,128)(2,1)S(1)} %get-tuple-element.82), channel_id=1, source_target_pairs={{8,0},{0,8},{24,16},{16,24},{9,1},{1,9},{25,17},{17,25},{10,2},{2,... | collective-permute-start | bytes 589832 | tf_op jit(solution)/shard_map/ppermute | solution.py:236
  71.6 10.2 %collective-permute-start.19 = (bf16[8,96,128]{2,1,0:T(8,128)(2,1)S(1)}, bf16[8,96,128]{2,1,0:T(8,128)(2,1)S(1)}, u32[]{:S(2)}, u32[]{:S(2)}) collective-permute-start(bf16[8,96,128]{2,1,0:T(8,128)(2,1)S(1)} %get-tuple-element.83), channel_id=1, source_target_pairs={{16,0},{24,8},{0,16},{8,24},{17,1},{25,9},{1,17},{9,25},{18,2},{26... | collective-permute-start | bytes 589832 | tf_op jit(solution)/shard_map/ppermute | solution.py:236
  72.5 9.3 %collective-permute-start.20 = (bf16[8,96,128]{2,1,0:T(8,128)(2,1)S(1)}, bf16[8,96,128]{2,1,0:T(8,128)(2,1)S(1)}, u32[]{:S(2)}, u32[]{:S(2)}) collective-permute-start(bf16[8,96,128]{2,1,0:T(8,128)(2,1)S(1)} %get-tuple-element.84), channel_id=1, source_target_pairs={{24,0},{16,8},{8,16},{0,24},{25,1},{17,9},{9,17},{1,25},{26,2},{18... | collective-permute-start | bytes 589832 | tf_op jit(solution)/shard_map/ppermute | solution.py:236
  74.4 7.4 %copy-start.1 = (bf16[16,256,192]{1,2,0:T(8,128)(2,1)S(1)}, bf16[16,256,192]{1,2,0:T(8,128)(2,1)}, u32[]{:S(2)}) copy-start(bf16[16,256,192]{1,2,0:T(8,128)(2,1)} %param.11) | copy-start | bytes 4718596
where the time goes:
time: 86 us; the launch traced here: 85.7 us
  Pallas kernels  42.1 us (49%)
  waiting for transfers between devices  20.8 us (24%)
  starting transfers between devices  19.7 us (23%)
  local copies, waits for them, and re-layouts  2.37 us (3%)
    ppermute x21, waiting for transfers between devices, shift(): return lax.ppermute(value, axis, pairs)  20.8 us
    ppermute x21, starting transfers between devices, shift(): return lax.ppermute(value, axis, pairs)  19.7 us
    pallas_call x1, Pallas kernels, parent_top(): pl.pallas_call(parent_top_kernel, out_shape=(jax.ShapeDtypeStruct(transfe...  12.6 us
    pallas_call x1, Pallas kernels, parent_low(): pl.pallas_call(parent_low_kernel, out_shape=jax.ShapeDtypeStruct(transfer...  11.1 us
    pallas_call x1, Pallas kernels, leaf_stage(): pl.pallas_call(functools.partial(leaf_kernel, leaves), in_specs=[smem, sm...  6.99 us
    pallas_call x2, Pallas kernels, serve(): pl.pallas_call(functools.partial(serve_kernel, size, span), in_specs=[sme...  4.55 us
    pallas_call x1, Pallas kernels, far_stage(): pl.pallas_call(functools.partial(far_kernel, groups, size, len(tables)),...  3.91 us
    pallas_call x1, Pallas kernels, near_stage(): pl.pallas_call(functools.partial(near_kernel, size), in_specs=[smem, smem...  2.87 us
  transfers between devices with their start and end apart: 21, of which 7 were waited for; matrix products, arithmetic and copies ran while one was open for 0% of the time, Pallas kernels for 42%

commit v1 on v0

--- a/solution.py
+++ b/solution.py
@@ -10,7 +10,7 @@
 SLAB = 64
 PANEL = 8
 STRIP = 32
-FIRST = 10
+FIRST = 9
 AHEAD = 4
 VMEM_LIMIT = 24 * 1024 * 1024
 
@@ -102,31 +102,51 @@
                 work[b * size + below : (b + 1) * size, :] = rest - dot(left, right, TN)[below:]
 
 
-def leaf_kernel(leaves, group, leaf_of, basis, code, rows_out, *rest):
+def leaf_kernel(basis, rows_out, kept_out, *rest):
     pieces, work = rest[:-1], rest[-1]
     count, points, rank = basis.shape
-
-    def pack(b, carry):
-        code[b] = group[b] * leaves + leaf_of[b]
-        return carry
-
-    lax.fori_loop(0, code.shape[0], pack, 0)
     for b in range(count):
         leaf = basis[b]
         work[b * rank : (b + 1) * rank, :] = dot(leaf, leaf, TN)
     factor(work, count, rank)
     for b in range(count):
-        high, low = split(lower_part(work[b * rank : (b + 1) * rank, :]))
-        leaf = basis[b]
-        value = (dot(leaf, high, NT) + dot(leaf, low, NT)).astype(rows_out.dtype)
+        value = orthonormal(work[b * rank : (b + 1) * rank, :], basis[b]).astype(rows_out.dtype)
         rows_out[b] = value
-        for span, piece in zip(points_split(points), pieces):
-            piece[b] = value[span]
-
-
-def parent_top_kernel(own_basis, own_transfer, far_basis, far_transfer, weighted, top, cross, corner):
+        if b < kept_out.shape[0]:
+            kept_out[b] = value
+            for span, piece in zip(points_split(points), pieces):
+                piece[b] = value[span]
+
+
+def orthonormal(factored, leaf):
+    high, low = split(lower_part(factored))
+    return dot(leaf, high, NT) + dot(leaf, low, NT)
+
+
+def extra_bases(batch, bases, rows, out, work):
+    early, points, rank = bases[0].shape
+    row = lax.broadcasted_iota(jnp.int32, (rank, rank), 0)
+    column = lax.broadcasted_iota(jnp.int32, (rank, rank), 1)
+    held = rows.shape[0]
+    for b in range(held):
+        out[b] = rows[b]
+    for first in range(0, out.shape[0] - held, batch):
+        last = min(first + batch, out.shape[0] - held)
+        leaves = [bases[n // early][n % early] for n in range(first, last)]
+        for b in range(batch):
+            gram = dot(leaves[b], leaves[b], TN) if b < len(leaves) else jnp.where(row == column, 1.0, 0.0)
+            work[b * rank : (b + 1) * rank, :] = gram
+        factor(work, batch, rank)
+        for b, leaf in enumerate(leaves):
+            value = orthonormal(work[b * rank : (b + 1) * rank, :], leaf)
+            out[held + first + b] = value.astype(out.dtype)
+
+
+def parent_top_kernel(own_basis, own_transfer, far_basis, far_transfer, rows, *refs):
+    bases, (weighted, top, cross, corner, combined, work) = refs[:-6], refs[-6:]
     count, points, rank = own_basis.shape
     half = own_transfer.shape[2] // 2
+    extra_bases(count, bases, rows, combined, work)
     for j in range(count):
         other = (j + count // 2) % count
         total = None
@@ -172,27 +192,25 @@
         out[j, :, half:] = dot_split(split(rest), inverse, NT)
 
 
-def leaf_stage(leaf_basis, leaves, group, leaf_of):
+def leaf_stage(leaf_basis, kept):
     count, points, rank = leaf_basis.shape
-    smem, vmem = pl.BlockSpec(memory_space=pltpu.SMEM), pl.BlockSpec(memory_space=pltpu.VMEM)
-    parts = [points] + [span.stop - span.start for span in points_split(points)]
+    shapes = [(count, points), (kept, points)]
+    shapes += [(kept, span.stop - span.start) for span in points_split(points)]
     return pl.pallas_call(
-        functools.partial(leaf_kernel, leaves),
-        in_specs=[smem, smem, vmem],
-        out_specs=[smem] + [vmem] * (len(parts) + 1),
-        out_shape=[jax.ShapeDtypeStruct(leaf_of.shape, jnp.int32)]
-        + [jax.ShapeDtypeStruct((count, part, rank), jnp.bfloat16) for part in parts]
+        leaf_kernel,
+        out_shape=[jax.ShapeDtypeStruct(shape + (rank,), jnp.bfloat16) for shape in shapes]
         + [jax.ShapeDtypeStruct((count * rank, rank), jnp.float32)],
         compiler_params=params(),
         cost_estimate=cost(10**9, 25 * 10**6),
         name="leaf_factor",
-    )(group, leaf_of, leaf_basis)
-
-
-def parent_top(leaf_basis, transfer, far_basis, far_transfer):
+    )(leaf_basis)
+
+
+def parent_top(leaf_basis, transfer, far_basis, far_transfer, rows, raw):
     count, points, rank = leaf_basis.shape
     half = transfer.shape[2] // 2
     square = jax.ShapeDtypeStruct((count, half, half), jnp.float32)
+    combined = (count + len(raw) * raw[0].shape[0], points, rank)
     return pl.pallas_call(
         parent_top_kernel,
         out_shape=(
@@ -200,11 +218,13 @@
             jax.ShapeDtypeStruct((count * half, half), jnp.float32),
             square,
             square,
+            jax.ShapeDtypeStruct(combined, jnp.bfloat16),
         ),
+        scratch_shapes=[pltpu.VMEM((count * rank, rank), jnp.float32)],
         compiler_params=params(),
-        cost_estimate=cost(10**9, 46 * 10**6),
+        cost_estimate=cost(10**9, 70 * 10**6),
         name="parent_top",
-    )(leaf_basis, transfer, far_basis, far_transfer)
+    )(leaf_basis, transfer, far_basis, far_transfer, rows, *raw)
 
 
 def parent_low(transfer, leaf_work, halves):
@@ -236,6 +256,10 @@
     return lax.ppermute(value, axis, pairs)
 
 
+def early_of(count):
+    return count // 4
+
+
 def joined(values, bit):
     return jnp.concatenate([values, shift(values, "clus", bit)], axis=0)
 
@@ -250,20 +274,30 @@
 
 
 def pick(table, leaf, span, store):
-    count = table[0].shape[0]
+    size, kept = len(table), table[2].shape[0]
+    early = (table[0].shape[0] - kept) // (size // 2)
+    count = kept + early
     place = quotient(leaf, count) ^ lax.axis_index("blk")
-    for d in range(len(table)):
-
-        @pl.when(place == d)
+    local = remainder(leaf, count)
+    here = (place < 2) | (local >= kept)
+    index = jnp.where(place < 2, local, count + ((place >> 1) - 1) * early + local - kept)
+    for d in range(size):
+
+        @pl.when((here & (place & 1 == d)) if d < 2 else (jnp.logical_not(here) & (place == d)))
         def _():
             rows = span if table[d].shape[1] > span.stop - span.start else slice(None)
-            store(table[d][remainder(leaf, count), rows, :])
+            store(table[d][index if d < 2 else local, rows, :])
+
+
+def leaves_of(table):
+    size, kept = len(table), table[2].shape[0]
+    return size * (kept + (table[0].shape[0] - kept) // (size // 2))
 
 
 def serve_kernel(size, span, asked, *refs):
     table, outs = refs[:size], refs[size:]
     me = lax.axis_index("clus")
-    leaves = size * table[0].shape[0]
+    leaves = leaves_of(table)
     for d in range(1, asked.shape[0]):
 
         def place(b, position, d=d):
@@ -340,7 +374,7 @@
     table, refs = refs[: chunks * size], refs[chunks * size :]
     fetched, (factors, out, held, tally) = refs[: chunks * (groups - 1)], refs[chunks * (groups - 1) :]
     count, width, points = factors.shape
-    leaves = size * table[0].shape[0]
+    leaves = leaves_of(table[:size])
     spans = points_split(points)
     me = lax.axis_index("clus")
     for g in range(groups):
@@ -406,40 +440,44 @@
 ):
     groups, size = lax.axis_size("clus"), lax.axis_size("blk")
     capacity = max(2, 2 * block_rows.shape[0] // groups)
-    spans = points_split(leaf_basis.shape[1])
+    count, points, _ = leaf_basis.shape
+    kept = count - early_of(count)
+    spans = points_split(points)
     barrier = lax.optimization_barrier
+    code = col_group[:, 0] * (count * size) + col_leaf
+    far_transfer = shift(transfer, "blk", 1)
     far_basis = shift(leaf_basis, "blk", 1)
-    far_transfer = shift(transfer, "blk", 1)
-    code, rows, first, second, leaf_work = leaf_stage(
-        leaf_basis, leaf_basis.shape[0] * size, col_group[:, 0], col_leaf
-    )
-    code, rows, first, second, far_basis, far_transfer = barrier(
-        (code, rows, first, second, far_basis, far_transfer)
+    raw = [shift(leaf_basis[kept:], "blk", d) for d in range(2, size, 2)]
+    rows, kept_rows, first, second, leaf_work = leaf_stage(leaf_basis, kept)
+    rows, kept_rows, first, second, far_basis, far_transfer, raw, code = barrier(
+        (rows, kept_rows, first, second, far_basis, far_transfer, raw, code)
     )
     chips = range(4, size, 2)
     table = {d: shift(first, "blk", d) for d in reversed(chips)}
-    close = {0: rows, 1: shift(rows, "blk", 1), 2: shift(rows, "blk", 2)}
+    table[2], table[3] = shift(kept_rows, "blk", 2), shift(kept_rows, "blk", 3)
     asked = joined(code[None], 1)
-    halves = parent_top(leaf_basis, transfer, far_basis, far_transfer)
-    asked, close[1], second, halves = barrier((asked, close[1], second, halves))
-    later = {d: shift(second, "blk", d) for d in reversed(chips)}
+    *halves, own = parent_top(leaf_basis, transfer, far_basis, far_transfer, rows, raw)
+    table, asked, halves, own, second = barrier((table, asked, halves, own, second))
     bit = 2
     while bit < groups:
         asked = joined(asked, bit)
         bit *= 2
-    transfer_new = parent_low(transfer, leaf_work, halves)
-    table, close, asked, transfer_new = barrier((table, close, asked, transfer_new))
+    later = {d: shift(second, "blk", d) for d in reversed(chips)}
     for d in chips:
         table[d + 1] = shift(table[d], "blk", 1)
-    close[3] = shift(close[2], "blk", 1)
-    served = serve(asked, in_order(close | table), spans[0], capacity)
+    table[0], table[1] = own, shift(own, "blk", 1)
+    served = serve(asked, in_order(table), spans[0], capacity)
+    served, halves = barrier((served, halves))
     fetched = [[shift(value, "clus", d + 1) for d, value in enumerate(served)]]
+    transfer_new = parent_low(transfer, leaf_work, halves)
+    later, transfer_new = barrier((later, transfer_new))
     for d in chips:
         later[d + 1] = shift(later[d], "blk", 1)
     later, fetched[0] = barrier((later, fetched[0]))
-    served = serve(asked, in_order(close | later), spans[1], capacity)
+    later = {**table, **later}
+    served = serve(asked, in_order(later), spans[1], capacity)
     fetched.append([shift(value, "clus", d + 1) for d, value in enumerate(served)])
-    tables = [in_order(close | table), in_order(close | later)]
+    tables = [in_order(table), in_order(later)]
     near = near_stage(row_leaf, rank_slabs, tables, jnp.swapaxes(block_rows, 1, 2))
     coupling = far_stage(asked[0], rank_slabs, near, tables, fetched, jnp.swapaxes(block_cols, 1, 2))
     return (coupling, transfer_new)

time: 86 us -> 93.4 us (1.086)
  starting transfers between devices: 19.7 us -> 24.6 us
  Pallas kernels: 42.1 us -> 45.9 us
  waiting for transfers between devices: 20.8 us -> 19.3 us
    pallas_call x1, Pallas kernels: 12.6 us -> 18.5 us  [parent_top(): pl.pallas_call(parent_top_kernel, out_shape=(jax.ShapeDtypeStruct(transfe...]
    ppermute x21 -> x24, starting transfers between devices: 19.7 us -> 24.6 us  [shift(): return lax.ppermute(value, axis, pairs)]
    ppermute x21 -> x24, waiting for transfers between devices: 20.8 us -> 19.3 us  [shift(): return lax.ppermute(value, axis, pairs)]
    unnamed x16 -> x12, local copies, waits for them, and re-layouts: 2.37 us -> 1.06 us
    pallas_call x1, Pallas kernels: 6.99 us -> 5.93 us  [leaf_stage(): pl.pallas_call(leaf_kernel, out_shape=[jax.ShapeDtypeStruct(shape + (rank...]
  transfers between devices with their start and end apart: 21 -> 24, of which waited for: 7 -> 7; matrix products, arithmetic and copies ran while one was open for 0% -> 2% of each run, Pallas kernels for 42% -> 44%
where the time goes in v1:
time: 93.4 us; the launch traced here: 93.3 us
  Pallas kernels  45.9 us (49%)
  starting transfers between devices  24.6 us (26%)
  waiting for transfers between devices  19.3 us (21%)
  local copies, waits for them, and re-layouts  1.98 us (2%)
    ppermute x24, starting transfers between devices, shift(): return lax.ppermute(value, axis, pairs)  24.6 us
    ppermute x24, waiting for transfers between devices, shift(): return lax.ppermute(value, axis, pairs)  19.3 us
    pallas_call x1, Pallas kernels, parent_top(): pl.pallas_call(parent_top_kernel, out_shape=(jax.ShapeDtypeStruct(transfe...  18.5 us
    pallas_call x1, Pallas kernels, parent_low(): pl.pallas_call(parent_low_kernel, out_shape=jax.ShapeDtypeStruct(transfer...  11.1 us
    pallas_call x1, Pallas kernels, leaf_stage(): pl.pallas_call(leaf_kernel, out_shape=[jax.ShapeDtypeStruct(shape + (rank...  5.93 us
    pallas_call x2, Pallas kernels, serve(): pl.pallas_call(functools.partial(serve_kernel, size, span), in_specs=[sme...  3.71 us
    pallas_call x1, Pallas kernels, far_stage(): pl.pallas_call(functools.partial(far_kernel, groups, size, len(tables)),...  3.57 us
    pallas_call x1, Pallas kernels, near_stage(): pl.pallas_call(functools.partial(near_kernel, size), in_specs=[smem, smem...  3.07 us
  transfers between devices with their start and end apart: 24, of which 7 were waited for; matrix products, arithmetic and copies ran while one was open for 2% of the time, Pallas kernels for 44%

profile of v1, /device:TPU:0, one launch (start us, length us, event | category | flops | bytes accessed | tf_op | source)
XLA Modules:
  0.0 93.3 jit_solution(640719059405984301)
XLA Ops:
  0.6 0.5 collective-permute-start.1
  1.1 0.1 collective-permute-start
  1.2 0.9 slice.8
  2.1 3.1 %collective-permute-start.2 = (bf16[2,256,128]{2,1,0:T(8,128)(2,1)S(1)}, bf16[2,256,128]{2,1,0:T(8,128)(2,1)S(1)}, u32[]{:S(2)}, u32[]{:S(2)}) collective-permute-start(bf16[2,256,128]{2,1,0:T(8,128)(2,1)S(1)} %slice.8), channel_id=1, source_target_pairs={{2,0},{3,1},{0,2},{1,3},{6,4},{7,5},{4,6},{5,7},{10,8},{11,9},{8,1... | collective-permute-start | bytes 393224 | tf_op jit(solution)/shard_map/ppermute | solution.py:256
  5.2 2.6 %collective-permute-start.3 = (bf16[2,256,128]{2,1,0:T(8,128)(2,1)S(1)}, bf16[2,256,128]{2,1,0:T(8,128)(2,1)S(1)}, u32[]{:S(2)}, u32[]{:S(2)}) collective-permute-start(bf16[2,256,128]{2,1,0:T(8,128)(2,1)S(1)} %slice.8), channel_id=1, source_target_pairs={{4,0},{5,1},{6,2},{7,3},{0,4},{1,5},{2,6},{3,7},{12,8},{13,9},{14,... | collective-permute-start | bytes 393224 | tf_op jit(solution)/shard_map/ppermute | solution.py:256
  7.8 0.0 collective-permute-start.4
  7.8 0.7 bitcast_add_fusion
  8.5 1.0 %copy-done.3 = bf16[8,256,128]{2,1,0:T(8,128)(2,1)S(1)} copy-done((bf16[8,256,128]{2,1,0:T(8,128)(2,1)S(1)}, bf16[8,256,128]{2,1,0:T(8,128)(2,1)}, u32[]{:S(2)}) %copy-start.3) | copy-done | bytes 524312
  9.5 5.9 %leaf_factor.1 = (bf16[8,256,128]{2,1,0:T(8,128)(2,1)S(1)}, bf16[6,256,128]{2,1,0:T(8,128)(2,1)S(1)}, bf16[6,144,128]{2,1,0:T(8,128)(2,1)S(1)}, bf16[6,112,128]{2,1,0:T(8,128)(2,1)S(1)}, f32[1024,128]{1,0:T(8,128)S(1)}) custom-call(bf16[8,256,128]{2,1,0:T(8,128)(2,1)S(1)} %copy-done.3), custom_call_target="tpu_custom_call" | custom-call | flops 1000000000 | bytes 25000000 | tf_op jit(solution)/shard_map/leaf_factor/pallas_call | solution.py:199
  15.5 0.0 collective-permute-done.2.refs_0_
  15.5 2.6 %collective-permute-done.3.refs_1_ = bf16[2,256,128]{2,1,0:T(8,128)(2,1)S(1)} collective-permute-done((bf16[2,256,128]{2,1,0:T(8,128)(2,1)S(1)}, bf16[2,256,128]{2,1,0:T(8,128)(2,1)S(1)}, u32[]{:S(2)}, u32[]{:S(2)}) %collective-permute-start.3) | collective-permute-done | bytes 131104 | tf_op jit(solution)/shard_map/ppermute | solution.py:256
  18.1 0.0 collective-permute-done.4.refs_2_
  18.1 0.0 collective-permute-done.far_basis
  18.1 0.0 collective-permute-done.1.far_transfer
  18.1 2.2 %collective-permute-start.5 = (bf16[6,256,128]{2,1,0:T(8,128)(2,1)S(1)}, bf16[6,256,128]{2,1,0:T(8,128)(2,1)S(1)}, u32[]{:S(2)}, u32[]{:S(2)}) collective-permute-start(bf16[6,256,128]{2,1,0:T(8,128)(2,1)S(1)} %get-tuple-element.60), channel_id=1, source_target_pairs={{2,0},{3,1},{0,2},{1,3},{6,4},{7,5},{4,6},{5,7},{10,8},{11,9},{8,1... | collective-permute-start | bytes 1179656 | tf_op jit(solution)/shard_map/ppermute | solution.py:256
  20.4 0.0 collective-permute-start.6
  20.4 1.4 %collective-permute-start.7 = (bf16[6,144,128]{2,1,0:T(8,128)(2,1)S(1)}, bf16[6,144,128]{2,1,0:T(8,128)(2,1)S(1)}, u32[]{:S(2)}, u32[]{:S(2)}) collective-permute-start(bf16[6,144,128]{2,1,0:T(8,128)(2,1)S(1)} %get-tuple-element.61), channel_id=1, source_target_pairs={{4,0},{5,1},{6,2},{7,3},{0,4},{1,5},{2,6},{3,7},{12,8},{13,9},{14,... | collective-permute-start | bytes 663560 | tf_op jit(solution)/shard_map/ppermute | solution.py:256
  21.7 1.3 %collective-permute-start.8 = (bf16[6,144,128]{2,1,0:T(8,128)(2,1)S(1)}, bf16[6,144,128]{2,1,0:T(8,128)(2,1)S(1)}, u32[]{:S(2)}, u32[]{:S(2)}) collective-permute-start(bf16[6,144,128]{2,1,0:T(8,128)(2,1)S(1)} %get-tuple-element.61), channel_id=1, source_target_pairs={{6,0},{7,1},{4,2},{5,3},{2,4},{3,5},{0,6},{1,7},{14,8},{15,9},{12,... | collective-permute-start | bytes 663560 | tf_op jit(solution)/shard_map/ppermute | solution.py:256
  23.0 1.5 %collective-permute-start.9 = (s32[1,16]{1,0:T(1,128)S(1)}, s32[1,16]{1,0:T(1,128)S(1)}, u32[]{:S(2)}, u32[]{:S(2)}) collective-permute-start(s32[1,16]{1,0:T(1,128)S(1)} %bitcast.9), channel_id=1, source_target_pairs={{8,0},{0,8},{24,16},{16,24},{9,1},{1,9},{25,17},{17,25},{10,2},{2,... | collective-permute-start | bytes 200 | tf_op jit(solution)/shard_map/ppermute | solution.py:256
  24.5 18.5 %parent_top.1 = (f32[8,128,256]{2,1,0:T(8,128)S(1)}, f32[1024,128]{1,0:T(8,128)S(1)}, f32[8,128,128]{2,1,0:T(8,128)S(1)}, f32[8,128,128]{2,1,0:T(8,128)S(1)}, bf16[14,256,128]{2,1,0:T(8,128)(2,1)S(1)}) custom-call(bf16[8,256,128]{2,1,0:T(8,128)(2,1)S(1)} %copy-done.3, f32[8,128,256]{2,1,0:T(8,128)S(1)} %copy-done.2, ...), custom_call_target="tpu_custom_call" | custom-call | flops 1000000000 | bytes 70000000 | tf_op jit(solution)/shard_map/parent_top/pallas_call | solution.py:214
  43.1 0.0 collective-permute-done.7.refs_4_
  43.1 5.7 %collective-permute-done.8.refs_6_ = bf16[6,144,128]{2,1,0:T(8,128)(2,1)S(1)} collective-permute-done((bf16[6,144,128]{2,1,0:T(8,128)(2,1)S(1)}, bf16[6,144,128]{2,1,0:T(8,128)(2,1)S(1)}, u32[]{:S(2)}, u32[]{:S(2)}) %collective-permute-start.8) | collective-permute-done | bytes 221216 | tf_op jit(solution)/shard_map/ppermute | solution.py:256
  48.8 0.0 collective-permute-done.6.refs_3_.refs_11_
  48.8 0.0 collective-permute-start.10
  48.8 0.5 collective-permute-start.11
  49.3 0.1 collective-permute-start.12
  49.3 1.5 %collective-permute-start.15 = (s32[2,16]{1,0:T(2,128)S(1)}, s32[2,16]{1,0:T(2,128)S(1)}, u32[]{:S(2)}, u32[]{:S(2)}) collective-permute-start(s32[2,16]{1,0:T(2,128)S(1)} %pad_add_fusion.1), channel_id=1, source_target_pairs={{16,0},{24,8},{0,16},{8,24},{17,1},{25,9},{1,17},{9,25},{18,2},{26... | collective-permute-start | bytes 392 | tf_op jit(solution)/shard_map/ppermute | solution.py:256
  50.9 2.0 %collective-permute-done.15 = s32[2,16]{1,0:T(2,128)S(1)} collective-permute-done((s32[2,16]{1,0:T(2,128)S(1)}, s32[2,16]{1,0:T(2,128)S(1)}, u32[]{:S(2)}, u32[]{:S(2)}) %collective-permute-start.15) | collective-permute-done | bytes 160 | tf_op jit(solution)/shard_map/ppermute | solution.py:256
  52.9 1.3 %collective-permute-start.14 = (bf16[6,112,128]{2,1,0:T(8,128)(2,1)S(1)}, bf16[6,112,128]{2,1,0:T(8,128)(2,1)S(1)}, u32[]{:S(2)}, u32[]{:S(2)}) collective-permute-start(bf16[6,112,128]{2,1,0:T(8,128)(2,1)S(1)} %get-tuple-element.81), channel_id=1, source_target_pairs={{6,0},{7,1},{4,2},{5,3},{2,4},{3,5},{0,6},{1,7},{14,8},{15,9},{12,... | collective-permute-start | bytes 516104 | tf_op jit(solution)/shard_map/ppermute | solution.py:256
  54.2 0.0 collective-permute-done.12.refs_7_
  54.2 2.0 %serve.2 = (bf16[8,144,128]{2,1,0:T(8,128)(2,1)S(1)}, bf16[8,144,128]{2,1,0:T(8,128)(2,1)S(1)}, bf16[8,144,128]{2,1,0:T(8,128)(2,1)S(1)}) custom-call(s32[4,16]{1,0:T(4,128)S(1)} %pad_add_fusion.asked, bf16[14,256,128]{2,1,0:T(8,128)(2,1)S(1)} %get-tuple-element.76.refs_0_.refs_8_, bf16[14,256,128]{2,1,0:T(8,128)(2,1)S(1)} %collective-permute-done.10.refs_1_.refs_9_, ...), custom_call_target="tpu_custom_call" | custom-call | flops 1000000000 | bytes 6000000 | tf_op jit(solution)/shard_map/serve/pallas_call | solution.py:323
  56.2 1.6 %collective-permute-start.18 = (bf16[8,144,128]{2,1,0:T(8,128)(2,1)S(1)}, bf16[8,144,128]{2,1,0:T(8,128)(2,1)S(1)}, u32[]{:S(2)}, u32[]{:S(2)}) collective-permute-start(bf16[8,144,128]{2,1,0:T(8,128)(2,1)S(1)} %get-tuple-element.96), channel_id=1, source_target_pairs={{8,0},{0,8},{24,16},{16,24},{9,1},{1,9},{25,17},{17,25},{10,2},{2,... | collective-permute-start | bytes 884744 | tf_op jit(solution)/shard_map/ppermute | solution.py:256
  57.8 2.2 %collective-permute-start.19 = (bf16[8,144,128]{2,1,0:T(8,128)(2,1)S(1)}, bf16[8,144,128]{2,1,0:T(8,128)(2,1)S(1)}, u32[]{:S(2)}, u32[]{:S(2)}) collective-permute-start(bf16[8,144,128]{2,1,0:T(8,128)(2,1)S(1)} %get-tuple-element.97), channel_id=1, source_target_pairs={{16,0},{24,8},{0,16},{8,24},{17,1},{25,9},{1,17},{9,25},{18,2},{26... | collective-permute-start | bytes 884744 | tf_op jit(solution)/shard_map/ppermute | solution.py:256
  60.0 11.1 %parent_low.1 = f32[8,128,256]{2,1,0:T(8,128)} custom-call(f32[1024,128]{1,0:T(8,128)S(1)} %get-tuple-element.82.leaf_work, f32[8,128,256]{2,1,0:T(8,128)S(1)} %get-tuple-element.90.weighted, f32[1024,128]{1,0:T(8,128)S(1)} %get-tuple-element.91.top, f32[8,128,128]{2,1,0:T(8,128)S(1)} %get-tuple-element.92.cross, f32[8,128,128]{2,1,0:T(8,128)S(1)} %get-tuple-element.93.corner), custom_call_target="tpu_custom_call" | custom-call | flops 1000000000 | bytes 40000000 | tf_op jit(solution)/shard_map/parent_low/pallas_call | solution.py:233
  71.1 0.0 collective-permute-done.14.refs_14_.refs_6_
  71.1 0.1 collective-permute-start.16
  71.2 0.5 collective-permute-start.17
  71.7 0.9 collective-permute-done.16.refs_13_.refs_5_
  72.6 0.2 collective-permute-done.17.refs_15_.refs_7_
  72.9 1.7 %serve.3 = (bf16[8,112,128]{2,1,0:T(8,128)(2,1)S(1)}, bf16[8,112,128]{2,1,0:T(8,128)(2,1)S(1)}, bf16[8,112,128]{2,1,0:T(8,128)(2,1)S(1)}) custom-call(s32[4,16]{1,0:T(4,128)S(1)} %pad_add_fusion.asked, bf16[14,256,128]{2,1,0:T(8,128)(2,1)S(1)} %get-tuple-element.76.refs_0_.refs_8_, bf16[14,256,128]{2,1,0:T(8,128)(2,1)S(1)} %collective-permute-done.10.refs_1_.refs_9_, ...), custom_call_target="tpu_custom_call" | custom-call | flops 1000000000 | bytes 6000000 | tf_op jit(solution)/shard_map/serve/pallas_call | solution.py:323
  74.6 1.6 %collective-permute-start.21 = (bf16[8,112,128]{2,1,0:T(8,128)(2,1)S(1)}, bf16[8,112,128]{2,1,0:T(8,128)(2,1)S(1)}, u32[]{:S(2)}, u32[]{:S(2)}) collective-permute-start(bf16[8,112,128]{2,1,0:T(8,128)(2,1)S(1)} %get-tuple-element.106), channel_id=1, source_target_pairs={{8,0},{0,8},{24,16},{16,24},{9,1},{1,9},{25,17},{17,25},{10,2},{2,... | collective-permute-start | bytes 688136 | tf_op jit(solution)/shard_map/ppermute | solution.py:256
  76.2 2.7 %collective-permute-start.22 = (bf16[8,112,128]{2,1,0:T(8,128)(2,1)S(1)}, bf16[8,112,128]{2,1,0:T(8,128)(2,1)S(1)}, u32[]{:S(2)}, u32[]{:S(2)}) collective-permute-start(bf16[8,112,128]{2,1,0:T(8,128)(2,1)S(1)} %get-tuple-element.107), channel_id=1, source_target_pairs={{16,0},{24,8},{0,16},{8,24},{17,1},{25,9},{1,17},{9,25},{18,2},{26... | collective-permute-start | bytes 688136 | tf_op jit(solution)/shard_map/ppermute | solution.py:256
  78.9 0.0 copy-start.1
  78.9 3.1 %near.1 = bf16[16,128,192]{2,1,0:T(8,128)(2,1)S(1)} custom-call(s32[16]{0:T(128)S(1)} %copy-done.5, s32[16]{0:T(128)S(1)} %copy-done.4, bf16[14,256,128]{2,1,0:T(8,128)(2,1)S(1)} %get-tuple-element.76.refs_0_.refs_8_, bf16[14,256,128]{2,1,0:T(8,128)(2,1)S(1)} %collective-permute-done.10.refs_1_.refs_9_, ...), custom_call_target="tpu_custom_call" | custom-call | flops 1000000000 | bytes 10000000 | tf_op jit(solution)/shard_map/near/pallas_call | solution.py:361
  82.0 1.2 %collective-permute-done.21.refs_19_ = bf16[8,112,128]{2,1,0:T(8,128)(2,1)S(1)} collective-permute-done((bf16[8,112,128]{2,1,0:T(8,128)(2,1)S(1)}, bf16[8,112,128]{2,1,0:T(8,128)(2,1)S(1)}, u32[]{:S(2)}, u32[]{:S(2)}) %collective-permute-start.21) | collective-permute-done | bytes 229408 | tf_op jit(solution)/shard_map/ppermute | solution.py:256
  83.1 6.6 %collective-permute-done.22.refs_20_ = bf16[8,112,128]{2,1,0:T(8,128)(2,1)S(1)} collective-permute-done((bf16[8,112,128]{2,1,0:T(8,128)(2,1)S(1)}, bf16[8,112,128]{2,1,0:T(8,128)(2,1)S(1)}, u32[]{:S(2)}, u32[]{:S(2)}) %collective-permute-start.22) | collective-permute-done | bytes 229408 | tf_op jit(solution)/shard_map/ppermute | solution.py:256
  89.7 0.0 collective-permute-done.23.refs_21_
  89.7 3.6 %far.1 = f32[16,128,128]{2,1,0:T(8,128)} custom-call(s32[16]{0:T(128)S(1)} %slice_bitcast_fusion.code, s32[16]{0:T(128)S(1)} %copy-done.4, bf16[16,128,192]{2,1,0:T(8,128)(2,1)S(1)} %near.1, bf16[14,256,128]{2,1,0:T(8,128)(2,1)S(1)} %get-tuple-element.76.refs_0_.refs_8_, bf16[14,256,128]{2,1,0:T(8,128)(2,1)S(1)} %collective-permute-done.10.refs_1_.refs_9_, ...), custom_call_target="tpu_custom_call" | custom-call | flops 1000000000 | bytes 13000000 | tf_op jit(solution)/shard_map/far/pallas_call | solution.py:423
  (24 shorter events, 0.1 us)
Async XLA Ops:
  0.6 17.5 %collective-permute-start.1 = (f32[8,128,256]{2,1,0:T(8,128)}, f32[8,128,256]{2,1,0:T(8,128)S(1)}, u32[]{:S(2)}, u32[]{:S(2)}) collective-permute-start(f32[8,128,256]{2,1,0:T(8,128)} %own_transfer.1), channel_id=1, source_target_pairs={{1,0},{0,1},{3,2},{2,3},{5,4},{4,5},{7,6},{6,7},{9,8},{8,9},{11,10... | collective-permute-start | bytes 3145736 | tf_op jit(solution)/shard_map/ppermute | solution.py:256
  1.1 17.0 %collective-permute-start = (bf16[8,256,128]{2,1,0:T(8,128)(2,1)}, bf16[8,256,128]{2,1,0:T(8,128)(2,1)S(1)}, u32[]{:S(2)}, u32[]{:S(2)}) collective-permute-start(bf16[8,256,128]{2,1,0:T(8,128)(2,1)} %own_basis.1), channel_id=1, source_target_pairs={{1,0},{0,1},{3,2},{2,3},{5,4},{4,5},{7,6},{6,7},{9,8},{8,9},{11,10... | collective-permute-start | bytes 1572872 | tf_op jit(solution)/shard_map/ppermute | solution.py:256
  2.1 13.3 %collective-permute-start.2 = (bf16[2,256,128]{2,1,0:T(8,128)(2,1)S(1)}, bf16[2,256,128]{2,1,0:T(8,128)(2,1)S(1)}, u32[]{:S(2)}, u32[]{:S(2)}) collective-permute-start(bf16[2,256,128]{2,1,0:T(8,128)(2,1)S(1)} %slice.8), channel_id=1, source_target_pairs={{2,0},{3,1},{0,2},{1,3},{6,4},{7,5},{4,6},{5,7},{10,8},{11,9},{8,1... | collective-permute-start | bytes 393224 | tf_op jit(solution)/shard_map/ppermute | solution.py:256
  5.2 12.9 %collective-permute-start.3 = (bf16[2,256,128]{2,1,0:T(8,128)(2,1)S(1)}, bf16[2,256,128]{2,1,0:T(8,128)(2,1)S(1)}, u32[]{:S(2)}, u32[]{:S(2)}) collective-permute-start(bf16[2,256,128]{2,1,0:T(8,128)(2,1)S(1)} %slice.8), channel_id=1, source_target_pairs={{4,0},{5,1},{6,2},{7,3},{0,4},{1,5},{2,6},{3,7},{12,8},{13,9},{14,... | collective-permute-start | bytes 393224 | tf_op jit(solution)/shard_map/ppermute | solution.py:256
  7.8 10.3 %collective-permute-start.4 = (bf16[2,256,128]{2,1,0:T(8,128)(2,1)S(1)}, bf16[2,256,128]{2,1,0:T(8,128)(2,1)S(1)}, u32[]{:S(2)}, u32[]{:S(2)}) collective-permute-start(bf16[2,256,128]{2,1,0:T(8,128)(2,1)S(1)} %slice.8), channel_id=1, source_target_pairs={{6,0},{7,1},{4,2},{5,3},{2,4},{3,5},{0,6},{1,7},{14,8},{15,9},{12,... | collective-permute-start | bytes 393224 | tf_op jit(solution)/shard_map/ppermute | solution.py:256
  8.5 1.0 %copy-start.3 = (bf16[8,256,128]{2,1,0:T(8,128)(2,1)S(1)}, bf16[8,256,128]{2,1,0:T(8,128)(2,1)}, u32[]{:S(2)}) copy-start(bf16[8,256,128]{2,1,0:T(8,128)(2,1)} %own_basis.1) | copy-start | bytes 1572868
  9.5 15.0 %copy-start.2 = (f32[8,128,256]{2,1,0:T(8,128)S(1)}, f32[8,128,256]{2,1,0:T(8,128)}, u32[]{:S(2)}) copy-start(f32[8,128,256]{2,1,0:T(8,128)} %own_transfer.1) | copy-start | bytes 3145732
  18.1 30.6 %collective-permute-start.5 = (bf16[6,256,128]{2,1,0:T(8,128)(2,1)S(1)}, bf16[6,256,128]{2,1,0:T(8,128)(2,1)S(1)}, u32[]{:S(2)}, u32[]{:S(2)}) collective-permute-start(bf16[6,256,128]{2,1,0:T(8,128)(2,1)S(1)} %get-tuple-element.60), channel_id=1, source_target_pairs={{2,0},{3,1},{0,2},{1,3},{6,4},{7,5},{4,6},{5,7},{10,8},{11,9},{8,1... | collective-permute-start | bytes 1179656 | tf_op jit(solution)/shard_map/ppermute | solution.py:256
  20.4 28.4 %collective-permute-start.6 = (bf16[6,256,128]{2,1,0:T(8,128)(2,1)S(1)}, bf16[6,256,128]{2,1,0:T(8,128)(2,1)S(1)}, u32[]{:S(2)}, u32[]{:S(2)}) collective-permute-start(bf16[6,256,128]{2,1,0:T(8,128)(2,1)S(1)} %get-tuple-element.60), channel_id=1, source_target_pairs={{3,0},{2,1},{1,2},{0,3},{7,4},{6,5},{5,6},{4,7},{11,8},{10,9},{9,1... | collective-permute-start | bytes 1179656 | tf_op jit(solution)/shard_map/ppermute | solution.py:256
  20.4 22.7 %collective-permute-start.7 = (bf16[6,144,128]{2,1,0:T(8,128)(2,1)S(1)}, bf16[6,144,128]{2,1,0:T(8,128)(2,1)S(1)}, u32[]{:S(2)}, u32[]{:S(2)}) collective-permute-start(bf16[6,144,128]{2,1,0:T(8,128)(2,1)S(1)} %get-tuple-element.61), channel_id=1, source_target_pairs={{4,0},{5,1},{6,2},{7,3},{0,4},{1,5},{2,6},{3,7},{12,8},{13,9},{14,... | collective-permute-start | bytes 663560 | tf_op jit(solution)/shard_map/ppermute | solution.py:256
  21.7 27.0 %collective-permute-start.8 = (bf16[6,144,128]{2,1,0:T(8,128)(2,1)S(1)}, bf16[6,144,128]{2,1,0:T(8,128)(2,1)S(1)}, u32[]{:S(2)}, u32[]{:S(2)}) collective-permute-start(bf16[6,144,128]{2,1,0:T(8,128)(2,1)S(1)} %get-tuple-element.61), channel_id=1, source_target_pairs={{6,0},{7,1},{4,2},{5,3},{2,4},{3,5},{0,6},{1,7},{14,8},{15,9},{12,... | collective-permute-start | bytes 663560 | tf_op jit(solution)/shard_map/ppermute | solution.py:256
  23.0 20.0 %collective-permute-start.9 = (s32[1,16]{1,0:T(1,128)S(1)}, s32[1,16]{1,0:T(1,128)S(1)}, u32[]{:S(2)}, u32[]{:S(2)}) collective-permute-start(s32[1,16]{1,0:T(1,128)S(1)} %bitcast.9), channel_id=1, source_target_pairs={{8,0},{0,8},{24,16},{16,24},{9,1},{1,9},{25,17},{17,25},{10,2},{2,... | collective-permute-start | bytes 200 | tf_op jit(solution)/shard_map/ppermute | solution.py:256
  48.8 5.5 %collective-permute-start.10 = (bf16[14,256,128]{2,1,0:T(8,128)(2,1)S(1)}, bf16[14,256,128]{2,1,0:T(8,128)(2,1)S(1)}, u32[]{:S(2)}, u32[]{:S(2)}) collective-permute-start(bf16[14,256,128]{2,1,0:T(8,128)(2,1)S(1)} %get-tuple-element.76.refs_0_.refs_8_), channel_id=1, source_target_pairs={{1,0},{0,1},{3,2},{2,3},{5,4},{4,5},{7,6},{6,7},{9,8},{8,9},{11,10... | collective-permute-start | bytes 2752520 | tf_op jit(solution)/shard_map/ppermute | solution.py:256
  48.8 5.5 %collective-permute-start.11 = (bf16[6,144,128]{2,1,0:T(8,128)(2,1)S(1)}, bf16[6,144,128]{2,1,0:T(8,128)(2,1)S(1)}, u32[]{:S(2)}, u32[]{:S(2)}) collective-permute-start(bf16[6,144,128]{2,1,0:T(8,128)(2,1)S(1)} %collective-permute-done.7.refs_4_), channel_id=1, source_target_pairs={{1,0},{0,1},{3,2},{2,3},{5,4},{4,5},{7,6},{6,7},{9,8},{8,9},{11,10... | collective-permute-start | bytes 663560 | tf_op jit(solution)/shard_map/ppermute | solution.py:256
  49.3 5.0 %collective-permute-start.12 = (bf16[6,144,128]{2,1,0:T(8,128)(2,1)S(1)}, bf16[6,144,128]{2,1,0:T(8,128)(2,1)S(1)}, u32[]{:S(2)}, u32[]{:S(2)}) collective-permute-start(bf16[6,144,128]{2,1,0:T(8,128)(2,1)S(1)} %collective-permute-done.8.refs_6_), channel_id=1, source_target_pairs={{1,0},{0,1},{3,2},{2,3},{5,4},{4,5},{7,6},{6,7},{9,8},{8,9},{11,10... | collective-permute-start | bytes 663560 | tf_op jit(solution)/shard_map/ppermute | solution.py:256
  49.3 3.6 %collective-permute-start.15 = (s32[2,16]{1,0:T(2,128)S(1)}, s32[2,16]{1,0:T(2,128)S(1)}, u32[]{:S(2)}, u32[]{:S(2)}) collective-permute-start(s32[2,16]{1,0:T(2,128)S(1)} %pad_add_fusion.1), channel_id=1, source_target_pairs={{16,0},{24,8},{0,16},{8,24},{17,1},{25,9},{1,17},{9,25},{18,2},{26... | collective-permute-start | bytes 392 | tf_op jit(solution)/shard_map/ppermute | solution.py:256
  50.9 20.3 %collective-permute-start.13 = (bf16[6,112,128]{2,1,0:T(8,128)(2,1)S(1)}, bf16[6,112,128]{2,1,0:T(8,128)(2,1)S(1)}, u32[]{:S(2)}, u32[]{:S(2)}) collective-permute-start(bf16[6,112,128]{2,1,0:T(8,128)(2,1)S(1)} %get-tuple-element.81), channel_id=1, source_target_pairs={{4,0},{5,1},{6,2},{7,3},{0,4},{1,5},{2,6},{3,7},{12,8},{13,9},{14,... | collective-permute-start | bytes 516104 | tf_op jit(solution)/shard_map/ppermute | solution.py:256
  52.9 18.2 %collective-permute-start.14 = (bf16[6,112,128]{2,1,0:T(8,128)(2,1)S(1)}, bf16[6,112,128]{2,1,0:T(8,128)(2,1)S(1)}, u32[]{:S(2)}, u32[]{:S(2)}) collective-permute-start(bf16[6,112,128]{2,1,0:T(8,128)(2,1)S(1)} %get-tuple-element.81), channel_id=1, source_target_pairs={{6,0},{7,1},{4,2},{5,3},{2,4},{3,5},{0,6},{1,7},{14,8},{15,9},{12,... | collective-permute-start | bytes 516104 | tf_op jit(solution)/shard_map/ppermute | solution.py:256
  56.2 16.6 %collective-permute-start.18 = (bf16[8,144,128]{2,1,0:T(8,128)(2,1)S(1)}, bf16[8,144,128]{2,1,0:T(8,128)(2,1)S(1)}, u32[]{:S(2)}, u32[]{:S(2)}) collective-permute-start(bf16[8,144,128]{2,1,0:T(8,128)(2,1)S(1)} %get-tuple-element.96), channel_id=1, source_target_pairs={{8,0},{0,8},{24,16},{16,24},{9,1},{1,9},{25,17},{17,25},{10,2},{2,... | collective-permute-start | bytes 884744 | tf_op jit(solution)/shard_map/ppermute | solution.py:256
  57.8 15.0 %collective-permute-start.19 = (bf16[8,144,128]{2,1,0:T(8,128)(2,1)S(1)}, bf16[8,144,128]{2,1,0:T(8,128)(2,1)S(1)}, u32[]{:S(2)}, u32[]{:S(2)}) collective-permute-start(bf16[8,144,128]{2,1,0:T(8,128)(2,1)S(1)} %get-tuple-element.97), channel_id=1, source_target_pairs={{16,0},{24,8},{0,16},{8,24},{17,1},{25,9},{1,17},{9,25},{18,2},{26... | collective-permute-start | bytes 884744 | tf_op jit(solution)/shard_map/ppermute | solution.py:256
  60.0 12.9 %collective-permute-start.20 = (bf16[8,144,128]{2,1,0:T(8,128)(2,1)S(1)}, bf16[8,144,128]{2,1,0:T(8,128)(2,1)S(1)}, u32[]{:S(2)}, u32[]{:S(2)}) collective-permute-start(bf16[8,144,128]{2,1,0:T(8,128)(2,1)S(1)} %get-tuple-element.98), channel_id=1, source_target_pairs={{24,0},{16,8},{8,16},{0,24},{25,1},{17,9},{9,17},{1,25},{26,2},{18... | collective-permute-start | bytes 884744 | tf_op jit(solution)/shard_map/ppermute | solution.py:256
  71.1 7.7 %copy-start = (bf16[16,256,192]{1,2,0:T(8,128)(2,1)S(1)}, bf16[16,256,192]{1,2,0:T(8,128)(2,1)}, u32[]{:S(2)}) copy-start(bf16[16,256,192]{1,2,0:T(8,128)(2,1)} %param.10) | copy-start | bytes 4718596
  71.1 7.7 %copy-start.4 = (s32[16]{0:T(128)S(1)}, s32[16]{0:T(128)}, u32[]{:S(2)}) copy-start(s32[16]{0:T(128)} %slabs.3) | copy-start | bytes 196
  71.1 7.8 %copy-start.5 = (s32[16]{0:T(128)S(1)}, s32[16]{0:T(128)}, u32[]{:S(2)}) copy-start(s32[16]{0:T(128)} %leaf.1) | copy-start | bytes 196
  71.1 1.5 %collective-permute-start.16 = (bf16[6,112,128]{2,1,0:T(8,128)(2,1)S(1)}, bf16[6,112,128]{2,1,0:T(8,128)(2,1)S(1)}, u32[]{:S(2)}, u32[]{:S(2)}) collective-permute-start(bf16[6,112,128]{2,1,0:T(8,128)(2,1)S(1)} %collective-permute-done.13.refs_12_.refs_4_), channel_id=1, source_target_pairs={{1,0},{0,1},{3,2},{2,3},{5,4},{4,5},{7,6},{6,7},{9,8},{8,9},{11,10... | collective-permute-start | bytes 516104 | tf_op jit(solution)/shard_map/ppermute | solution.py:256
  71.2 1.6 %collective-permute-start.17 = (bf16[6,112,128]{2,1,0:T(8,128)(2,1)S(1)}, bf16[6,112,128]{2,1,0:T(8,128)(2,1)S(1)}, u32[]{:S(2)}, u32[]{:S(2)}) collective-permute-start(bf16[6,112,128]{2,1,0:T(8,128)(2,1)S(1)} %collective-permute-done.14.refs_14_.refs_6_), channel_id=1, source_target_pairs={{1,0},{0,1},{3,2},{2,3},{5,4},{4,5},{7,6},{6,7},{9,8},{8,9},{11,10... | collective-permute-start | bytes 516104 | tf_op jit(solution)/shard_map/ppermute | solution.py:256
  74.6 8.5 %collective-permute-start.21 = (bf16[8,112,128]{2,1,0:T(8,128)(2,1)S(1)}, bf16[8,112,128]{2,1,0:T(8,128)(2,1)S(1)}, u32[]{:S(2)}, u32[]{:S(2)}) collective-permute-start(bf16[8,112,128]{2,1,0:T(8,128)(2,1)S(1)} %get-tuple-element.106), channel_id=1, source_target_pairs={{8,0},{0,8},{24,16},{16,24},{9,1},{1,9},{25,17},{17,25},{10,2},{2,... | collective-permute-start | bytes 688136 | tf_op jit(solution)/shard_map/ppermute | solution.py:256
  76.2 13.5 %collective-permute-start.22 = (bf16[8,112,128]{2,1,0:T(8,128)(2,1)S(1)}, bf16[8,112,128]{2,1,0:T(8,128)(2,1)S(1)}, u32[]{:S(2)}, u32[]{:S(2)}) collective-permute-start(bf16[8,112,128]{2,1,0:T(8,128)(2,1)S(1)} %get-tuple-element.107), channel_id=1, source_target_pairs={{16,0},{24,8},{0,16},{8,24},{17,1},{25,9},{1,17},{9,25},{18,2},{26... | collective-permute-start | bytes 688136 | tf_op jit(solution)/shard_map/ppermute | solution.py:256
  78.8 10.8 %collective-permute-start.23 = (bf16[8,112,128]{2,1,0:T(8,128)(2,1)S(1)}, bf16[8,112,128]{2,1,0:T(8,128)(2,1)S(1)}, u32[]{:S(2)}, u32[]{:S(2)}) collective-permute-start(bf16[8,112,128]{2,1,0:T(8,128)(2,1)S(1)} %get-tuple-element.108), channel_id=1, source_target_pairs={{24,0},{16,8},{8,16},{0,24},{25,1},{17,9},{9,17},{1,25},{26,2},{18... | collective-permute-start | bytes 688136 | tf_op jit(solution)/shard_map/ppermute | solution.py:256
  78.9 10.8 %copy-start.1 = (bf16[16,256,192]{1,2,0:T(8,128)(2,1)S(1)}, bf16[16,256,192]{1,2,0:T(8,128)(2,1)}, u32[]{:S(2)}) copy-start(bf16[16,256,192]{1,2,0:T(8,128)(2,1)} %param.11) | copy-start | bytes 4718596

commit v2 on v0

--- a/solution.py
+++ b/solution.py
@@ -102,15 +102,9 @@
                 work[b * size + below : (b + 1) * size, :] = rest - dot(left, right, TN)[below:]
 
 
-def leaf_kernel(leaves, group, leaf_of, basis, code, rows_out, *rest):
+def leaf_kernel(basis, rows_out, *rest):
     pieces, work = rest[:-1], rest[-1]
     count, points, rank = basis.shape
-
-    def pack(b, carry):
-        code[b] = group[b] * leaves + leaf_of[b]
-        return carry
-
-    lax.fori_loop(0, code.shape[0], pack, 0)
     for b in range(count):
         leaf = basis[b]
         work[b * rank : (b + 1) * rank, :] = dot(leaf, leaf, TN)
@@ -172,21 +166,17 @@
         out[j, :, half:] = dot_split(split(rest), inverse, NT)
 
 
-def leaf_stage(leaf_basis, leaves, group, leaf_of):
+def leaf_stage(leaf_basis):
     count, points, rank = leaf_basis.shape
-    smem, vmem = pl.BlockSpec(memory_space=pltpu.SMEM), pl.BlockSpec(memory_space=pltpu.VMEM)
     parts = [points] + [span.stop - span.start for span in points_split(points)]
     return pl.pallas_call(
-        functools.partial(leaf_kernel, leaves),
-        in_specs=[smem, smem, vmem],
-        out_specs=[smem] + [vmem] * (len(parts) + 1),
-        out_shape=[jax.ShapeDtypeStruct(leaf_of.shape, jnp.int32)]
-        + [jax.ShapeDtypeStruct((count, part, rank), jnp.bfloat16) for part in parts]
+        leaf_kernel,
+        out_shape=[jax.ShapeDtypeStruct((count, part, rank), jnp.bfloat16) for part in parts]
         + [jax.ShapeDtypeStruct((count * rank, rank), jnp.float32)],
         compiler_params=params(),
         cost_estimate=cost(10**9, 25 * 10**6),
         name="leaf_factor",
-    )(group, leaf_of, leaf_basis)
+    )(leaf_basis)
 
 
 def parent_top(leaf_basis, transfer, far_basis, far_transfer):
@@ -410,9 +400,8 @@
     barrier = lax.optimization_barrier
     far_basis = shift(leaf_basis, "blk", 1)
     far_transfer = shift(transfer, "blk", 1)
-    code, rows, first, second, leaf_work = leaf_stage(
-        leaf_basis, leaf_basis.shape[0] * size, col_group[:, 0], col_leaf
-    )
+    code = col_group[:, 0] * (leaf_basis.shape[0] * size) + col_leaf
+    rows, first, second, leaf_work = leaf_stage(leaf_basis)
     code, rows, first, second, far_basis, far_transfer = barrier(
         (code, rows, first, second, far_basis, far_transfer)
     )

time: 86 us -> 83.4 us (0.970)
  Pallas kernels: 42.1 us -> 39.5 us
  local copies, waits for them, and re-layouts: 2.37 us -> 1.07 us
  waiting for transfers between devices: 20.8 us -> 21.8 us
    unnamed x16, local copies, waits for them, and re-layouts: 2.37 us -> 1.07 us
    pallas_call x2, Pallas kernels: 4.55 us -> 3.46 us  [serve(): pl.pallas_call(functools.partial(serve_kernel, size, span), in_specs=[sme...]
    pallas_call x1, Pallas kernels: 6.99 us -> 5.91 us  [leaf_stage(): pl.pallas_call(leaf_kernel, out_shape=[jax.ShapeDtypeStruct((count, part,...]
    ppermute x21, waiting for transfers between devices: 20.8 us -> 21.8 us  [shift(): return lax.ppermute(value, axis, pairs)]
  transfers between devices with their start and end apart: 21 -> 21, of which waited for: 7 -> 9; matrix products, arithmetic and copies ran while one was open for 0% -> 0% of each run, Pallas kernels for 42% -> 41%
where the time goes in v2:
time: 83.4 us; the launch traced here: 83 us
  Pallas kernels  39.5 us (47%)
  waiting for transfers between devices  21.8 us (26%)
  starting transfers between devices  19.9 us (24%)
  local copies, waits for them, and re-layouts  1.07 us (1%)
    ppermute x21, waiting for transfers between devices, shift(): return lax.ppermute(value, axis, pairs)  21.8 us
    ppermute x21, starting transfers between devices, shift(): return lax.ppermute(value, axis, pairs)  19.9 us
    pallas_call x1, Pallas kernels, parent_top(): pl.pallas_call(parent_top_kernel, out_shape=(jax.ShapeDtypeStruct(transfe...  12.6 us
    pallas_call x1, Pallas kernels, parent_low(): pl.pallas_call(parent_low_kernel, out_shape=jax.ShapeDtypeStruct(transfer...  11.1 us
    pallas_call x1, Pallas kernels, leaf_stage(): pl.pallas_call(leaf_kernel, out_shape=[jax.ShapeDtypeStruct((count, part,...  5.91 us
    pallas_call x1, Pallas kernels, far_stage(): pl.pallas_call(functools.partial(far_kernel, groups, size, len(tables)),...  3.53 us
    pallas_call x2, Pallas kernels, serve(): pl.pallas_call(functools.partial(serve_kernel, size, span), in_specs=[sme...  3.46 us
    pallas_call x1, Pallas kernels, near_stage(): pl.pallas_call(functools.partial(near_kernel, size), in_specs=[smem, smem...  2.86 us
  transfers between devices with their start and end apart: 21, of which 9 were waited for; matrix products, arithmetic and copies ran while one was open for 0% of the time, Pallas kernels for 41%

profile of v2, /device:TPU:0, one launch (start us, length us, event | category | flops | bytes accessed | tf_op | source)
XLA Modules:
  0.0 83.0 jit_solution(12206172286200372654)
XLA Ops:
  0.6 0.5 collective-permute-start.1
  1.2 0.1 collective-permute-start
  1.2 1.0 %copy-done.5 = bf16[8,256,128]{2,1,0:T(8,128)(2,1)S(1)} copy-done((bf16[8,256,128]{2,1,0:T(8,128)(2,1)S(1)}, bf16[8,256,128]{2,1,0:T(8,128)(2,1)}, u32[]{:S(2)}) %copy-start.5) | copy-done | bytes 524312
  2.3 5.9 %leaf_factor.1 = (bf16[8,256,128]{2,1,0:T(8,128)(2,1)S(1)}, bf16[8,160,128]{2,1,0:T(8,128)(2,1)S(1)}, bf16[8,96,128]{2,1,0:T(8,128)(2,1)S(1)}, f32[1024,128]{1,0:T(8,128)S(1)}) custom-call(bf16[8,256,128]{2,1,0:T(8,128)(2,1)S(1)} %copy-done.5), custom_call_target="tpu_custom_call" | custom-call | flops 1000000000 | bytes 25000000 | tf_op jit(solution)/shard_map/leaf_factor/pallas_call | solution.py:172
  8.2 0.0 collective-permute-done.far_basis
  8.2 0.0 collective-permute-done.1.far_transfer
  8.3 0.5 collective-permute-start.5
  8.8 2.6 %collective-permute-start.6 = (bf16[8,256,128]{2,1,0:T(8,128)(2,1)S(1)}, bf16[8,256,128]{2,1,0:T(8,128)(2,1)S(1)}, u32[]{:S(2)}, u32[]{:S(2)}) collective-permute-start(bf16[8,256,128]{2,1,0:T(8,128)(2,1)S(1)} %get-tuple-element.64.refs_0_.refs_8_), channel_id=1, source_target_pairs={{2,0},{3,1},{0,2},{1,3},{6,4},{7,5},{4,6},{5,7},{10,8},{11,9},{8,1... | collective-permute-start | bytes 1572872 | tf_op jit(solution)/shard_map/ppermute | solution.py:226
  11.4 2.5 %collective-permute-start.3 = (bf16[8,160,128]{2,1,0:T(8,128)(2,1)S(1)}, bf16[8,160,128]{2,1,0:T(8,128)(2,1)S(1)}, u32[]{:S(2)}, u32[]{:S(2)}) collective-permute-start(bf16[8,160,128]{2,1,0:T(8,128)(2,1)S(1)} %get-tuple-element.46), channel_id=1, source_target_pairs={{6,0},{7,1},{4,2},{5,3},{2,4},{3,5},{0,6},{1,7},{14,8},{15,9},{12,... | collective-permute-start | bytes 983048 | tf_op jit(solution)/shard_map/ppermute | solution.py:226
  13.9 0.1 collective-permute-start.2
  14.0 1.5 %collective-permute-start.4 = (s32[1,16]{1,0:T(1,128)S(1)}, s32[1,16]{1,0:T(1,128)S(1)}, u32[]{:S(2)}, u32[]{:S(2)}) collective-permute-start(s32[1,16]{1,0:T(1,128)S(1)} %bitcast.9), channel_id=1, source_target_pairs={{8,0},{0,8},{24,16},{16,24},{9,1},{1,9},{25,17},{17,25},{10,2},{2,... | collective-permute-start | bytes 200 | tf_op jit(solution)/shard_map/ppermute | solution.py:226
  15.5 12.6 %parent_top.1 = (f32[8,128,256]{2,1,0:T(8,128)S(1)}, f32[1024,128]{1,0:T(8,128)S(1)}, f32[8,128,128]{2,1,0:T(8,128)S(1)}, f32[8,128,128]{2,1,0:T(8,128)S(1)}) custom-call(bf16[8,256,128]{2,1,0:T(8,128)(2,1)S(1)} %copy-done.5, f32[8,128,256]{2,1,0:T(8,128)S(1)} %copy-done.4, bf16[8,256,128]{2,1,0:T(8,128)(2,1)S(1)} %collective-permute-done.far_basis, ...), custom_call_target="tpu_custom_call" | custom-call | flops 1000000000 | bytes 46000000 | tf_op jit(solution)/shard_map/parent_top/pallas_call | solution.py:186
  28.1 0.0 collective-permute-done.4
  28.1 0.0 collective-permute-done.5.refs_1_.refs_9_
  28.2 1.6 %collective-permute-start.7 = (s32[2,16]{1,0:T(2,128)S(1)}, s32[2,16]{1,0:T(2,128)S(1)}, u32[]{:S(2)}, u32[]{:S(2)}) collective-permute-start(s32[2,16]{1,0:T(2,128)S(1)} %pad_add_fusion.1), channel_id=1, source_target_pairs={{16,0},{24,8},{0,16},{8,24},{17,1},{25,9},{1,17},{9,25},{18,2},{26... | collective-permute-start | bytes 392 | tf_op jit(solution)/shard_map/ppermute | solution.py:226
  29.8 11.1 %parent_low.1 = f32[8,128,256]{2,1,0:T(8,128)} custom-call(f32[1024,128]{1,0:T(8,128)S(1)} %get-tuple-element.58.leaf_work, f32[8,128,256]{2,1,0:T(8,128)S(1)} %get-tuple-element.59.weighted, f32[1024,128]{1,0:T(8,128)S(1)} %get-tuple-element.60.top, f32[8,128,128]{2,1,0:T(8,128)S(1)} %get-tuple-element.61.cross, f32[8,128,128]{2,1,0:T(8,128)S(1)} %get-tuple-element.62.corner), custom_call_target="tpu_custom_call" | custom-call | flops 1000000000 | bytes 40000000 | tf_op jit(solution)/shard_map/parent_low/pallas_call | solution.py:203
  40.9 0.0 collective-permute-done.7
  40.9 0.0 collective-permute-done.3.refs_6_
  40.9 2.2 %collective-permute-done.2.refs_4_ = bf16[8,160,128]{2,1,0:T(8,128)(2,1)S(1)} collective-permute-done((bf16[8,160,128]{2,1,0:T(8,128)(2,1)S(1)}, bf16[8,160,128]{2,1,0:T(8,128)(2,1)S(1)}, u32[]{:S(2)}, u32[]{:S(2)}) %collective-permute-start.2) | collective-permute-done | bytes 327712 | tf_op jit(solution)/shard_map/ppermute | solution.py:226
  43.2 0.0 collective-permute-done.6.refs_2_.refs_10_
  43.2 0.0 collective-permute-start.8
  43.2 0.5 collective-permute-start.9
  43.7 0.0 collective-permute-start.10
  43.7 2.6 %collective-permute-start.13 = (bf16[8,96,128]{2,1,0:T(8,128)(2,1)S(1)}, bf16[8,96,128]{2,1,0:T(8,128)(2,1)S(1)}, u32[]{:S(2)}, u32[]{:S(2)}) collective-permute-start(bf16[8,96,128]{2,1,0:T(8,128)(2,1)S(1)} %get-tuple-element.69), channel_id=1, source_target_pairs={{6,0},{7,1},{4,2},{5,3},{2,4},{3,5},{0,6},{1,7},{14,8},{15,9},{12,... | collective-permute-start | bytes 589832 | tf_op jit(solution)/shard_map/ppermute | solution.py:226
  46.3 0.0 collective-permute-start.11
  46.3 0.0 collective-permute-done.9.refs_5_
  46.3 0.0 collective-permute-done.10.refs_7_
  46.3 0.0 collective-permute-done.8.refs_3_.refs_11_
  46.3 1.7 %serve.2 = (bf16[8,160,128]{2,1,0:T(8,128)(2,1)S(1)}, bf16[8,160,128]{2,1,0:T(8,128)(2,1)S(1)}, bf16[8,160,128]{2,1,0:T(8,128)(2,1)S(1)}) custom-call(s32[4,16]{1,0:T(4,128)S(1)} %pad_add_fusion.asked, bf16[8,256,128]{2,1,0:T(8,128)(2,1)S(1)} %get-tuple-element.64.refs_0_.refs_8_, bf16[8,256,128]{2,1,0:T(8,128)(2,1)S(1)} %collective-permute-done.5.refs_1_.refs_9_, ...), custom_call_target="tpu_custom_call" | custom-call | flops 1000000000 | bytes 6000000 | tf_op jit(solution)/shard_map/serve/pallas_call | solution.py:279
  48.1 1.7 %collective-permute-start.15 = (bf16[8,160,128]{2,1,0:T(8,128)(2,1)S(1)}, bf16[8,160,128]{2,1,0:T(8,128)(2,1)S(1)}, u32[]{:S(2)}, u32[]{:S(2)}) collective-permute-start(bf16[8,160,128]{2,1,0:T(8,128)(2,1)S(1)} %get-tuple-element.70), channel_id=1, source_target_pairs={{8,0},{0,8},{24,16},{16,24},{9,1},{1,9},{25,17},{17,25},{10,2},{2,... | collective-permute-start | bytes 983048 | tf_op jit(solution)/shard_map/ppermute | solution.py:226
  49.8 1.4 %collective-permute-start.16 = (bf16[8,160,128]{2,1,0:T(8,128)(2,1)S(1)}, bf16[8,160,128]{2,1,0:T(8,128)(2,1)S(1)}, u32[]{:S(2)}, u32[]{:S(2)}) collective-permute-start(bf16[8,160,128]{2,1,0:T(8,128)(2,1)S(1)} %get-tuple-element.71), channel_id=1, source_target_pairs={{16,0},{24,8},{0,16},{8,24},{17,1},{25,9},{1,17},{9,25},{18,2},{26... | collective-permute-start | bytes 983048 | tf_op jit(solution)/shard_map/ppermute | solution.py:226
  51.1 0.7 collective-permute-start.17
  51.8 1.4 %collective-permute-done.13.refs_14_.refs_6_ = bf16[8,96,128]{2,1,0:T(8,128)(2,1)S(1)} collective-permute-done((bf16[8,96,128]{2,1,0:T(8,128)(2,1)S(1)}, bf16[8,96,128]{2,1,0:T(8,128)(2,1)S(1)}, u32[]{:S(2)}, u32[]{:S(2)}) %collective-permute-start.13) | collective-permute-done | bytes 196640 | tf_op jit(solution)/shard_map/ppermute | solution.py:226
  53.3 9.6 %collective-permute-done.11.refs_12_.refs_4_ = bf16[8,96,128]{2,1,0:T(8,128)(2,1)S(1)} collective-permute-done((bf16[8,96,128]{2,1,0:T(8,128)(2,1)S(1)}, bf16[8,96,128]{2,1,0:T(8,128)(2,1)S(1)}, u32[]{:S(2)}, u32[]{:S(2)}) %collective-permute-start.11) | collective-permute-done | bytes 196640 | tf_op jit(solution)/shard_map/ppermute | solution.py:226
  62.9 0.0 collective-permute-start.12
  62.9 1.4 %collective-permute-done.12.refs_13_.refs_5_ = bf16[8,96,128]{2,1,0:T(8,128)(2,1)S(1)} collective-permute-done((bf16[8,96,128]{2,1,0:T(8,128)(2,1)S(1)}, bf16[8,96,128]{2,1,0:T(8,128)(2,1)S(1)}, u32[]{:S(2)}, u32[]{:S(2)}) %collective-permute-start.12) | collective-permute-done | bytes 196640 | tf_op jit(solution)/shard_map/ppermute | solution.py:226
  64.3 0.9 %collective-permute-done.16.refs_17_ = bf16[8,160,128]{2,1,0:T(8,128)(2,1)S(1)} collective-permute-done((bf16[8,160,128]{2,1,0:T(8,128)(2,1)S(1)}, bf16[8,160,128]{2,1,0:T(8,128)(2,1)S(1)}, u32[]{:S(2)}, u32[]{:S(2)}) %collective-permute-start.16) | collective-permute-done | bytes 327712 | tf_op jit(solution)/shard_map/ppermute | solution.py:226
  65.2 1.3 %collective-permute-done.17.refs_18_ = bf16[8,160,128]{2,1,0:T(8,128)(2,1)S(1)} collective-permute-done((bf16[8,160,128]{2,1,0:T(8,128)(2,1)S(1)}, bf16[8,160,128]{2,1,0:T(8,128)(2,1)S(1)}, u32[]{:S(2)}, u32[]{:S(2)}) %collective-permute-start.17) | collective-permute-done | bytes 327712 | tf_op jit(solution)/shard_map/ppermute | solution.py:226
  66.5 1.7 %serve.3 = (bf16[8,96,128]{2,1,0:T(8,128)(2,1)S(1)}, bf16[8,96,128]{2,1,0:T(8,128)(2,1)S(1)}, bf16[8,96,128]{2,1,0:T(8,128)(2,1)S(1)}) custom-call(s32[4,16]{1,0:T(4,128)S(1)} %pad_add_fusion.asked, bf16[8,256,128]{2,1,0:T(8,128)(2,1)S(1)} %get-tuple-element.64.refs_0_.refs_8_, bf16[8,256,128]{2,1,0:T(8,128)(2,1)S(1)} %collective-permute-done.5.refs_1_.refs_9_, ...), custom_call_target="tpu_custom_call" | custom-call | flops 1000000000 | bytes 6000000 | tf_op jit(solution)/shard_map/serve/pallas_call | solution.py:279
  68.2 1.1 %collective-permute-start.18 = (bf16[8,96,128]{2,1,0:T(8,128)(2,1)S(1)}, bf16[8,96,128]{2,1,0:T(8,128)(2,1)S(1)}, u32[]{:S(2)}, u32[]{:S(2)}) collective-permute-start(bf16[8,96,128]{2,1,0:T(8,128)(2,1)S(1)} %get-tuple-element.80), channel_id=1, source_target_pairs={{8,0},{0,8},{24,16},{16,24},{9,1},{1,9},{25,17},{17,25},{10,2},{2,... | collective-permute-start | bytes 589832 | tf_op jit(solution)/shard_map/ppermute | solution.py:226
  69.3 1.3 %collective-permute-start.19 = (bf16[8,96,128]{2,1,0:T(8,128)(2,1)S(1)}, bf16[8,96,128]{2,1,0:T(8,128)(2,1)S(1)}, u32[]{:S(2)}, u32[]{:S(2)}) collective-permute-start(bf16[8,96,128]{2,1,0:T(8,128)(2,1)S(1)} %get-tuple-element.81), channel_id=1, source_target_pairs={{16,0},{24,8},{0,16},{8,24},{17,1},{25,9},{1,17},{9,25},{18,2},{26... | collective-permute-start | bytes 589832 | tf_op jit(solution)/shard_map/ppermute | solution.py:226
  70.6 1.2 %collective-permute-start.20 = (bf16[8,96,128]{2,1,0:T(8,128)(2,1)S(1)}, bf16[8,96,128]{2,1,0:T(8,128)(2,1)S(1)}, u32[]{:S(2)}, u32[]{:S(2)}) collective-permute-start(bf16[8,96,128]{2,1,0:T(8,128)(2,1)S(1)} %get-tuple-element.82), channel_id=1, source_target_pairs={{24,0},{16,8},{8,16},{0,24},{25,1},{17,9},{9,17},{1,25},{26,2},{18... | collective-permute-start | bytes 589832 | tf_op jit(solution)/shard_map/ppermute | solution.py:226
  71.8 0.0 copy-start.1
  71.8 2.9 %near.1 = bf16[16,128,192]{2,1,0:T(8,128)(2,1)S(1)} custom-call(s32[16]{0:T(128)S(1)} %copy-done.3, s32[16]{0:T(128)S(1)} %copy-done.2, bf16[8,256,128]{2,1,0:T(8,128)(2,1)S(1)} %get-tuple-element.64.refs_0_.refs_8_, bf16[8,256,128]{2,1,0:T(8,128)(2,1)S(1)} %collective-permute-done.5.refs_1_.refs_9_, ...), custom_call_target="tpu_custom_call" | custom-call | flops 1000000000 | bytes 10000000 | tf_op jit(solution)/shard_map/near/pallas_call | solution.py:317
  74.7 1.5 %collective-permute-done.18.refs_19_ = bf16[8,96,128]{2,1,0:T(8,128)(2,1)S(1)} collective-permute-done((bf16[8,96,128]{2,1,0:T(8,128)(2,1)S(1)}, bf16[8,96,128]{2,1,0:T(8,128)(2,1)S(1)}, u32[]{:S(2)}, u32[]{:S(2)}) %collective-permute-start.18) | collective-permute-done | bytes 196640 | tf_op jit(solution)/shard_map/ppermute | solution.py:226
  76.1 1.9 %collective-permute-done.19.refs_20_ = bf16[8,96,128]{2,1,0:T(8,128)(2,1)S(1)} collective-permute-done((bf16[8,96,128]{2,1,0:T(8,128)(2,1)S(1)}, bf16[8,96,128]{2,1,0:T(8,128)(2,1)S(1)}, u32[]{:S(2)}, u32[]{:S(2)}) %collective-permute-start.19) | collective-permute-done | bytes 196640 | tf_op jit(solution)/shard_map/ppermute | solution.py:226
  78.0 1.5 %collective-permute-done.20.refs_21_ = bf16[8,96,128]{2,1,0:T(8,128)(2,1)S(1)} collective-permute-done((bf16[8,96,128]{2,1,0:T(8,128)(2,1)S(1)}, bf16[8,96,128]{2,1,0:T(8,128)(2,1)S(1)}, u32[]{:S(2)}, u32[]{:S(2)}) %collective-permute-start.20) | collective-permute-done | bytes 196640 | tf_op jit(solution)/shard_map/ppermute | solution.py:226
  79.5 3.5 %far.1 = f32[16,128,128]{2,1,0:T(8,128)} custom-call(s32[16]{0:T(128)S(1)} %slice_bitcast_fusion.code, s32[16]{0:T(128)S(1)} %copy-done.2, bf16[16,128,192]{2,1,0:T(8,128)(2,1)S(1)} %near.1, bf16[8,256,128]{2,1,0:T(8,128)(2,1)S(1)} %get-tuple-element.64.refs_0_.refs_8_, bf16[8,256,128]{2,1,0:T(8,128)(2,1)S(1)} %collective-permute-done.5.refs_1_.refs_9_, ...), custom_call_target="tpu_custom_call" | custom-call | flops 1000000000 | bytes 13000000 | tf_op jit(solution)/shard_map/far/pallas_call | solution.py:379
  (21 shorter events, 0.1 us)
Async XLA Ops:
  0.6 14.9 %copy-start.4 = (f32[8,128,256]{2,1,0:T(8,128)S(1)}, f32[8,128,256]{2,1,0:T(8,128)}, u32[]{:S(2)}) copy-start(f32[8,128,256]{2,1,0:T(8,128)} %own_transfer.1) | copy-start | bytes 3145732
  0.6 7.6 %collective-permute-start.1 = (f32[8,128,256]{2,1,0:T(8,128)}, f32[8,128,256]{2,1,0:T(8,128)S(1)}, u32[]{:S(2)}, u32[]{:S(2)}) collective-permute-start(f32[8,128,256]{2,1,0:T(8,128)} %own_transfer.1), channel_id=1, source_target_pairs={{1,0},{0,1},{3,2},{2,3},{5,4},{4,5},{7,6},{6,7},{9,8},{8,9},{11,10... | collective-permute-start | bytes 3145736 | tf_op jit(solution)/shard_map/ppermute | solution.py:226
  1.2 7.1 %collective-permute-start = (bf16[8,256,128]{2,1,0:T(8,128)(2,1)}, bf16[8,256,128]{2,1,0:T(8,128)(2,1)S(1)}, u32[]{:S(2)}, u32[]{:S(2)}) collective-permute-start(bf16[8,256,128]{2,1,0:T(8,128)(2,1)} %own_basis.1), channel_id=1, source_target_pairs={{1,0},{0,1},{3,2},{2,3},{5,4},{4,5},{7,6},{6,7},{9,8},{8,9},{11,10... | collective-permute-start | bytes 1572872 | tf_op jit(solution)/shard_map/ppermute | solution.py:226
  1.2 1.0 %copy-start.5 = (bf16[8,256,128]{2,1,0:T(8,128)(2,1)S(1)}, bf16[8,256,128]{2,1,0:T(8,128)(2,1)}, u32[]{:S(2)}) copy-start(bf16[8,256,128]{2,1,0:T(8,128)(2,1)} %own_basis.1) | copy-start | bytes 1572868
  2.3 5.9 %copy-start.6 = (s32[16]{0:T(128)S(1)}, s32[16]{0:T(128)}, u32[]{:S(2)}) copy-start(s32[16]{0:T(128)} %param.15) | copy-start | bytes 196
  2.3 5.9 %copy-start.7 = (s32[16,1]{0,1:T(1,128)S(1)}, s32[16,1]{0,1:T(1,128)}, u32[]{:S(2)}) copy-start(s32[16,1]{0,1:T(1,128)} %param.14) | copy-start | bytes 196
  8.3 19.9 %collective-permute-start.5 = (bf16[8,256,128]{2,1,0:T(8,128)(2,1)S(1)}, bf16[8,256,128]{2,1,0:T(8,128)(2,1)S(1)}, u32[]{:S(2)}, u32[]{:S(2)}) collective-permute-start(bf16[8,256,128]{2,1,0:T(8,128)(2,1)S(1)} %get-tuple-element.64.refs_0_.refs_8_), channel_id=1, source_target_pairs={{1,0},{0,1},{3,2},{2,3},{5,4},{4,5},{7,6},{6,7},{9,8},{8,9},{11,10... | collective-permute-start | bytes 1572872 | tf_op jit(solution)/shard_map/ppermute | solution.py:226
  8.8 34.4 %collective-permute-start.6 = (bf16[8,256,128]{2,1,0:T(8,128)(2,1)S(1)}, bf16[8,256,128]{2,1,0:T(8,128)(2,1)S(1)}, u32[]{:S(2)}, u32[]{:S(2)}) collective-permute-start(bf16[8,256,128]{2,1,0:T(8,128)(2,1)S(1)} %get-tuple-element.64.refs_0_.refs_8_), channel_id=1, source_target_pairs={{2,0},{3,1},{0,2},{1,3},{6,4},{7,5},{4,6},{5,7},{10,8},{11,9},{8,1... | collective-permute-start | bytes 1572872 | tf_op jit(solution)/shard_map/ppermute | solution.py:226
  11.4 29.5 %collective-permute-start.3 = (bf16[8,160,128]{2,1,0:T(8,128)(2,1)S(1)}, bf16[8,160,128]{2,1,0:T(8,128)(2,1)S(1)}, u32[]{:S(2)}, u32[]{:S(2)}) collective-permute-start(bf16[8,160,128]{2,1,0:T(8,128)(2,1)S(1)} %get-tuple-element.46), channel_id=1, source_target_pairs={{6,0},{7,1},{4,2},{5,3},{2,4},{3,5},{0,6},{1,7},{14,8},{15,9},{12,... | collective-permute-start | bytes 983048 | tf_op jit(solution)/shard_map/ppermute | solution.py:226
  13.9 29.3 %collective-permute-start.2 = (bf16[8,160,128]{2,1,0:T(8,128)(2,1)S(1)}, bf16[8,160,128]{2,1,0:T(8,128)(2,1)S(1)}, u32[]{:S(2)}, u32[]{:S(2)}) collective-permute-start(bf16[8,160,128]{2,1,0:T(8,128)(2,1)S(1)} %get-tuple-element.46), channel_id=1, source_target_pairs={{4,0},{5,1},{6,2},{7,3},{0,4},{1,5},{2,6},{3,7},{12,8},{13,9},{14,... | collective-permute-start | bytes 983048 | tf_op jit(solution)/shard_map/ppermute | solution.py:226
  14.0 14.1 %collective-permute-start.4 = (s32[1,16]{1,0:T(1,128)S(1)}, s32[1,16]{1,0:T(1,128)S(1)}, u32[]{:S(2)}, u32[]{:S(2)}) collective-permute-start(s32[1,16]{1,0:T(1,128)S(1)} %bitcast.9), channel_id=1, source_target_pairs={{8,0},{0,8},{24,16},{16,24},{9,1},{1,9},{25,17},{17,25},{10,2},{2,... | collective-permute-start | bytes 200 | tf_op jit(solution)/shard_map/ppermute | solution.py:226
  28.2 12.7 %collective-permute-start.7 = (s32[2,16]{1,0:T(2,128)S(1)}, s32[2,16]{1,0:T(2,128)S(1)}, u32[]{:S(2)}, u32[]{:S(2)}) collective-permute-start(s32[2,16]{1,0:T(2,128)S(1)} %pad_add_fusion.1), channel_id=1, source_target_pairs={{16,0},{24,8},{0,16},{8,24},{17,1},{25,9},{1,17},{9,25},{18,2},{26... | collective-permute-start | bytes 392 | tf_op jit(solution)/shard_map/ppermute | solution.py:226
  43.2 3.2 %collective-permute-start.8 = (bf16[8,256,128]{2,1,0:T(8,128)(2,1)S(1)}, bf16[8,256,128]{2,1,0:T(8,128)(2,1)S(1)}, u32[]{:S(2)}, u32[]{:S(2)}) collective-permute-start(bf16[8,256,128]{2,1,0:T(8,128)(2,1)S(1)} %collective-permute-done.6.refs_2_.refs_10_), channel_id=1, source_target_pairs={{1,0},{0,1},{3,2},{2,3},{5,4},{4,5},{7,6},{6,7},{9,8},{8,9},{11,10... | collective-permute-start | bytes 1572872 | tf_op jit(solution)/shard_map/ppermute | solution.py:226
  43.2 3.2 %collective-permute-start.9 = (bf16[8,160,128]{2,1,0:T(8,128)(2,1)S(1)}, bf16[8,160,128]{2,1,0:T(8,128)(2,1)S(1)}, u32[]{:S(2)}, u32[]{:S(2)}) collective-permute-start(bf16[8,160,128]{2,1,0:T(8,128)(2,1)S(1)} %collective-permute-done.2.refs_4_), channel_id=1, source_target_pairs={{1,0},{0,1},{3,2},{2,3},{5,4},{4,5},{7,6},{6,7},{9,8},{8,9},{11,10... | collective-permute-start | bytes 983048 | tf_op jit(solution)/shard_map/ppermute | solution.py:226
  43.7 2.7 %collective-permute-start.10 = (bf16[8,160,128]{2,1,0:T(8,128)(2,1)S(1)}, bf16[8,160,128]{2,1,0:T(8,128)(2,1)S(1)}, u32[]{:S(2)}, u32[]{:S(2)}) collective-permute-start(bf16[8,160,128]{2,1,0:T(8,128)(2,1)S(1)} %collective-permute-done.3.refs_6_), channel_id=1, source_target_pairs={{1,0},{0,1},{3,2},{2,3},{5,4},{4,5},{7,6},{6,7},{9,8},{8,9},{11,10... | collective-permute-start | bytes 983048 | tf_op jit(solution)/shard_map/ppermute | solution.py:226
  43.7 9.6 %collective-permute-start.13 = (bf16[8,96,128]{2,1,0:T(8,128)(2,1)S(1)}, bf16[8,96,128]{2,1,0:T(8,128)(2,1)S(1)}, u32[]{:S(2)}, u32[]{:S(2)}) collective-permute-start(bf16[8,96,128]{2,1,0:T(8,128)(2,1)S(1)} %get-tuple-element.69), channel_id=1, source_target_pairs={{6,0},{7,1},{4,2},{5,3},{2,4},{3,5},{0,6},{1,7},{14,8},{15,9},{12,... | collective-permute-start | bytes 589832 | tf_op jit(solution)/shard_map/ppermute | solution.py:226
  46.3 16.6 %collective-permute-start.11 = (bf16[8,96,128]{2,1,0:T(8,128)(2,1)S(1)}, bf16[8,96,128]{2,1,0:T(8,128)(2,1)S(1)}, u32[]{:S(2)}, u32[]{:S(2)}) collective-permute-start(bf16[8,96,128]{2,1,0:T(8,128)(2,1)S(1)} %get-tuple-element.69), channel_id=1, source_target_pairs={{4,0},{5,1},{6,2},{7,3},{0,4},{1,5},{2,6},{3,7},{12,8},{13,9},{14,... | collective-permute-start | bytes 589832 | tf_op jit(solution)/shard_map/ppermute | solution.py:226
  48.1 16.3 %collective-permute-start.15 = (bf16[8,160,128]{2,1,0:T(8,128)(2,1)S(1)}, bf16[8,160,128]{2,1,0:T(8,128)(2,1)S(1)}, u32[]{:S(2)}, u32[]{:S(2)}) collective-permute-start(bf16[8,160,128]{2,1,0:T(8,128)(2,1)S(1)} %get-tuple-element.70), channel_id=1, source_target_pairs={{8,0},{0,8},{24,16},{16,24},{9,1},{1,9},{25,17},{17,25},{10,2},{2,... | collective-permute-start | bytes 983048 | tf_op jit(solution)/shard_map/ppermute | solution.py:226
  49.8 15.4 %collective-permute-start.16 = (bf16[8,160,128]{2,1,0:T(8,128)(2,1)S(1)}, bf16[8,160,128]{2,1,0:T(8,128)(2,1)S(1)}, u32[]{:S(2)}, u32[]{:S(2)}) collective-permute-start(bf16[8,160,128]{2,1,0:T(8,128)(2,1)S(1)} %get-tuple-element.71), channel_id=1, source_target_pairs={{16,0},{24,8},{0,16},{8,24},{17,1},{25,9},{1,17},{9,25},{18,2},{26... | collective-permute-start | bytes 983048 | tf_op jit(solution)/shard_map/ppermute | solution.py:226
  51.1 20.7 %copy-start = (bf16[16,256,192]{1,2,0:T(8,128)(2,1)S(1)}, bf16[16,256,192]{1,2,0:T(8,128)(2,1)}, u32[]{:S(2)}) copy-start(bf16[16,256,192]{1,2,0:T(8,128)(2,1)} %param.10) | copy-start | bytes 4718596
  51.1 20.7 %copy-start.2 = (s32[16]{0:T(128)S(1)}, s32[16]{0:T(128)}, u32[]{:S(2)}) copy-start(s32[16]{0:T(128)} %slabs.3) | copy-start | bytes 196
  51.1 20.7 %copy-start.3 = (s32[16]{0:T(128)S(1)}, s32[16]{0:T(128)}, u32[]{:S(2)}) copy-start(s32[16]{0:T(128)} %leaf.1) | copy-start | bytes 196
  51.1 15.4 %collective-permute-start.17 = (bf16[8,160,128]{2,1,0:T(8,128)(2,1)S(1)}, bf16[8,160,128]{2,1,0:T(8,128)(2,1)S(1)}, u32[]{:S(2)}, u32[]{:S(2)}) collective-permute-start(bf16[8,160,128]{2,1,0:T(8,128)(2,1)S(1)} %get-tuple-element.72), channel_id=1, source_target_pairs={{24,0},{16,8},{8,16},{0,24},{25,1},{17,9},{9,17},{1,25},{26,2},{18... | collective-permute-start | bytes 983048 | tf_op jit(solution)/shard_map/ppermute | solution.py:226
  53.3 9.6 %collective-permute-start.14 = (bf16[8,96,128]{2,1,0:T(8,128)(2,1)S(1)}, bf16[8,96,128]{2,1,0:T(8,128)(2,1)S(1)}, u32[]{:S(2)}, u32[]{:S(2)}) collective-permute-start(bf16[8,96,128]{2,1,0:T(8,128)(2,1)S(1)} %collective-permute-done.13.refs_14_.refs_6_), channel_id=1, source_target_pairs={{1,0},{0,1},{3,2},{2,3},{5,4},{4,5},{7,6},{6,7},{9,8},{8,9},{11,10... | collective-permute-start | bytes 589832 | tf_op jit(solution)/shard_map/ppermute | solution.py:226
  62.9 1.4 %collective-permute-start.12 = (bf16[8,96,128]{2,1,0:T(8,128)(2,1)S(1)}, bf16[8,96,128]{2,1,0:T(8,128)(2,1)S(1)}, u32[]{:S(2)}, u32[]{:S(2)}) collective-permute-start(bf16[8,96,128]{2,1,0:T(8,128)(2,1)S(1)} %collective-permute-done.11.refs_12_.refs_4_), channel_id=1, source_target_pairs={{1,0},{0,1},{3,2},{2,3},{5,4},{4,5},{7,6},{6,7},{9,8},{8,9},{11,10... | collective-permute-start | bytes 589832 | tf_op jit(solution)/shard_map/ppermute | solution.py:226
  68.2 7.9 %collective-permute-start.18 = (bf16[8,96,128]{2,1,0:T(8,128)(2,1)S(1)}, bf16[8,96,128]{2,1,0:T(8,128)(2,1)S(1)}, u32[]{:S(2)}, u32[]{:S(2)}) collective-permute-start(bf16[8,96,128]{2,1,0:T(8,128)(2,1)S(1)} %get-tuple-element.80), channel_id=1, source_target_pairs={{8,0},{0,8},{24,16},{16,24},{9,1},{1,9},{25,17},{17,25},{10,2},{2,... | collective-permute-start | bytes 589832 | tf_op jit(solution)/shard_map/ppermute | solution.py:226
  69.3 8.7 %collective-permute-start.19 = (bf16[8,96,128]{2,1,0:T(8,128)(2,1)S(1)}, bf16[8,96,128]{2,1,0:T(8,128)(2,1)S(1)}, u32[]{:S(2)}, u32[]{:S(2)}) collective-permute-start(bf16[8,96,128]{2,1,0:T(8,128)(2,1)S(1)} %get-tuple-element.81), channel_id=1, source_target_pairs={{16,0},{24,8},{0,16},{8,24},{17,1},{25,9},{1,17},{9,25},{18,2},{26... | collective-permute-start | bytes 589832 | tf_op jit(solution)/shard_map/ppermute | solution.py:226
  70.6 8.9 %collective-permute-start.20 = (bf16[8,96,128]{2,1,0:T(8,128)(2,1)S(1)}, bf16[8,96,128]{2,1,0:T(8,128)(2,1)S(1)}, u32[]{:S(2)}, u32[]{:S(2)}) collective-permute-start(bf16[8,96,128]{2,1,0:T(8,128)(2,1)S(1)} %get-tuple-element.82), channel_id=1, source_target_pairs={{24,0},{16,8},{8,16},{0,24},{25,1},{17,9},{9,17},{1,25},{26,2},{18... | collective-permute-start | bytes 589832 | tf_op jit(solution)/shard_map/ppermute | solution.py:226
  71.8 7.7 %copy-start.1 = (bf16[16,256,192]{1,2,0:T(8,128)(2,1)S(1)}, bf16[16,256,192]{1,2,0:T(8,128)(2,1)}, u32[]{:S(2)}) copy-start(bf16[16,256,192]{1,2,0:T(8,128)(2,1)} %param.11) | copy-start | bytes 4718596

commit v3 on v2

--- a/solution.py
+++ b/solution.py
@@ -239,15 +239,27 @@
     return (slice(0, first), slice(first, points))
 
 
+def choose(index, low, high, act):
+    if high - low == 1:
+        act(low)
+        return
+    middle = (low + high) // 2
+    lax.cond(
+        index < middle,
+        lambda: choose(index, low, middle, act),
+        lambda: choose(index, middle, high, act),
+    )
+
+
 def pick(table, leaf, span, store):
     count = table[0].shape[0]
-    place = quotient(leaf, count) ^ lax.axis_index("blk")
-    for d in range(len(table)):
-
-        @pl.when(place == d)
-        def _():
-            rows = span if table[d].shape[1] > span.stop - span.start else slice(None)
-            store(table[d][remainder(leaf, count), rows, :])
+    local = remainder(leaf, count)
+
+    def take(d):
+        rows = span if table[d].shape[1] > span.stop - span.start else slice(None)
+        store(table[d][local, rows, :])
+
+    choose(quotient(leaf, count) ^ lax.axis_index("blk"), 0, len(table), take)
 
 
 def serve_kernel(size, span, asked, *refs):
@@ -269,7 +281,7 @@
 
             return position + mine.astype(jnp.int32)
 
-        lax.fori_loop(0, asked.shape[1], place, jnp.int32(0))
+        lax.fori_loop(0, asked.shape[1], place, jnp.int32(0), unroll=4)
 
 
 def serve(asked, table, span, capacity):
@@ -342,23 +354,19 @@
         tally[group] = position + 1
         away = group ^ me
 
-        @pl.when(away == 0)
-        def _():
+        def take(d):
             for c in range(chunks):
-
-                def store(value, c=c):
-                    held[b, spans[c], :] = value
-
-                pick(table[c * size : (c + 1) * size], leaf, spans[c], store)
-
-        for d in range(1, groups):
-
-            @pl.when(away == d)
-            def _(d=d):
-                for c in range(chunks):
+                if d == 0:
+
+                    def store(value, c=c):
+                        held[b, spans[c], :] = value
+
+                    pick(table[c * size : (c + 1) * size], leaf, spans[c], store)
+                else:
                     piece = fetched[c * (groups - 1) + d - 1]
                     held[b, spans[c], :] = piece[position]
 
+        choose(away, 0, groups, take)
         return carry
 
     lax.fori_loop(0, count, gather, 0)

time: 83.4 us -> 82.6 us (level)
  Pallas kernels: 39.5 us -> 38.3 us
    ppermute x21, waiting for transfers between devices: 21.8 us -> 22.6 us  [shift(): return lax.ppermute(value, axis, pairs)]
  transfers between devices with their start and end apart: 21 -> 21, of which waited for: 9 -> 7; matrix products, arithmetic and copies ran while one was open for 0% -> 0% of each run, Pallas kernels for 41% -> 41%
where the time goes in v3:
time: 82.6 us; the launch traced here: 82.5 us
  Pallas kernels  38.3 us (46%)
  waiting for transfers between devices  22.6 us (27%)
  starting transfers between devices  19.7 us (24%)
  local copies, waits for them, and re-layouts  1.07 us (1%)
    ppermute x21, waiting for transfers between devices, shift(): return lax.ppermute(value, axis, pairs)  22.6 us
    ppermute x21, starting transfers between devices, shift(): return lax.ppermute(value, axis, pairs)  19.7 us
    pallas_call x1, Pallas kernels, parent_top(): pl.pallas_call(parent_top_kernel, out_shape=(jax.ShapeDtypeStruct(transfe...  12.6 us
    pallas_call x1, Pallas kernels, parent_low(): pl.pallas_call(parent_low_kernel, out_shape=jax.ShapeDtypeStruct(transfer...  11.1 us
    pallas_call x1, Pallas kernels, leaf_stage(): pl.pallas_call(leaf_kernel, out_shape=[jax.ShapeDtypeStruct((count, part,...  5.91 us
    pallas_call x1, Pallas kernels, far_stage(): pl.pallas_call(functools.partial(far_kernel, groups, size, len(tables)),...  3.39 us
    pallas_call x2, Pallas kernels, serve(): pl.pallas_call(functools.partial(serve_kernel, size, span), in_specs=[sme...  3.11 us
    pallas_call x1, Pallas kernels, near_stage(): pl.pallas_call(functools.partial(near_kernel, size), in_specs=[smem, smem...  2.15 us
  transfers between devices with their start and end apart: 21, of which 7 were waited for; matrix products, arithmetic and copies ran while one was open for 0% of the time, Pallas kernels for 41%

profile of v3, /device:TPU:0, one launch (start us, length us, event | category | flops | bytes accessed | tf_op | source)
XLA Modules:
  0.0 82.5 jit_solution(14321693552779771131)
XLA Ops:
  0.6 0.5 collective-permute-start.1
  1.2 0.1 collective-permute-start
  1.2 1.0 %copy-done.5 = bf16[8,256,128]{2,1,0:T(8,128)(2,1)S(1)} copy-done((bf16[8,256,128]{2,1,0:T(8,128)(2,1)S(1)}, bf16[8,256,128]{2,1,0:T(8,128)(2,1)}, u32[]{:S(2)}) %copy-start.5) | copy-done | bytes 524312
  2.3 5.9 %leaf_factor.1 = (bf16[8,256,128]{2,1,0:T(8,128)(2,1)S(1)}, bf16[8,160,128]{2,1,0:T(8,128)(2,1)S(1)}, bf16[8,96,128]{2,1,0:T(8,128)(2,1)S(1)}, f32[1024,128]{1,0:T(8,128)S(1)}) custom-call(bf16[8,256,128]{2,1,0:T(8,128)(2,1)S(1)} %copy-done.5), custom_call_target="tpu_custom_call" | custom-call | flops 1000000000 | bytes 25000000 | tf_op jit(solution)/shard_map/leaf_factor/pallas_call | solution.py:172
  8.2 0.0 collective-permute-done.far_basis
  8.2 0.0 collective-permute-done.1.far_transfer
  8.3 0.5 collective-permute-start.5
  8.8 2.6 %collective-permute-start.6 = (bf16[8,256,128]{2,1,0:T(8,128)(2,1)S(1)}, bf16[8,256,128]{2,1,0:T(8,128)(2,1)S(1)}, u32[]{:S(2)}, u32[]{:S(2)}) collective-permute-start(bf16[8,256,128]{2,1,0:T(8,128)(2,1)S(1)} %get-tuple-element.64.refs_0_.refs_8_), channel_id=1, source_target_pairs={{2,0},{3,1},{0,2},{1,3},{6,4},{7,5},{4,6},{5,7},{10,8},{11,9},{8,1... | collective-permute-start | bytes 1572872 | tf_op jit(solution)/shard_map/ppermute | solution.py:226
  11.4 2.5 %collective-permute-start.3 = (bf16[8,160,128]{2,1,0:T(8,128)(2,1)S(1)}, bf16[8,160,128]{2,1,0:T(8,128)(2,1)S(1)}, u32[]{:S(2)}, u32[]{:S(2)}) collective-permute-start(bf16[8,160,128]{2,1,0:T(8,128)(2,1)S(1)} %get-tuple-element.46), channel_id=1, source_target_pairs={{6,0},{7,1},{4,2},{5,3},{2,4},{3,5},{0,6},{1,7},{14,8},{15,9},{12,... | collective-permute-start | bytes 983048 | tf_op jit(solution)/shard_map/ppermute | solution.py:226
  13.9 0.1 collective-permute-start.2
  14.0 1.5 %collective-permute-start.4 = (s32[1,16]{1,0:T(1,128)S(1)}, s32[1,16]{1,0:T(1,128)S(1)}, u32[]{:S(2)}, u32[]{:S(2)}) collective-permute-start(s32[1,16]{1,0:T(1,128)S(1)} %bitcast.9), channel_id=1, source_target_pairs={{8,0},{0,8},{24,16},{16,24},{9,1},{1,9},{25,17},{17,25},{10,2},{2,... | collective-permute-start | bytes 200 | tf_op jit(solution)/shard_map/ppermute | solution.py:226
  15.5 12.6 %parent_top.1 = (f32[8,128,256]{2,1,0:T(8,128)S(1)}, f32[1024,128]{1,0:T(8,128)S(1)}, f32[8,128,128]{2,1,0:T(8,128)S(1)}, f32[8,128,128]{2,1,0:T(8,128)S(1)}) custom-call(bf16[8,256,128]{2,1,0:T(8,128)(2,1)S(1)} %copy-done.5, f32[8,128,256]{2,1,0:T(8,128)S(1)} %copy-done.4, bf16[8,256,128]{2,1,0:T(8,128)(2,1)S(1)} %collective-permute-done.far_basis, ...), custom_call_target="tpu_custom_call" | custom-call | flops 1000000000 | bytes 46000000 | tf_op jit(solution)/shard_map/parent_top/pallas_call | solution.py:186
  28.1 0.0 collective-permute-done.4
  28.1 0.0 collective-permute-done.5.refs_1_.refs_9_
  28.2 1.6 %collective-permute-start.7 = (s32[2,16]{1,0:T(2,128)S(1)}, s32[2,16]{1,0:T(2,128)S(1)}, u32[]{:S(2)}, u32[]{:S(2)}) collective-permute-start(s32[2,16]{1,0:T(2,128)S(1)} %pad_add_fusion.1), channel_id=1, source_target_pairs={{16,0},{24,8},{0,16},{8,24},{17,1},{25,9},{1,17},{9,25},{18,2},{26... | collective-permute-start | bytes 392 | tf_op jit(solution)/shard_map/ppermute | solution.py:226
  29.8 11.1 %parent_low.1 = f32[8,128,256]{2,1,0:T(8,128)} custom-call(f32[1024,128]{1,0:T(8,128)S(1)} %get-tuple-element.58.leaf_work, f32[8,128,256]{2,1,0:T(8,128)S(1)} %get-tuple-element.59.weighted, f32[1024,128]{1,0:T(8,128)S(1)} %get-tuple-element.60.top, f32[8,128,128]{2,1,0:T(8,128)S(1)} %get-tuple-element.61.cross, f32[8,128,128]{2,1,0:T(8,128)S(1)} %get-tuple-element.62.corner), custom_call_target="tpu_custom_call" | custom-call | flops 1000000000 | bytes 40000000 | tf_op jit(solution)/shard_map/parent_low/pallas_call | solution.py:203
  40.9 0.0 collective-permute-done.7
  40.9 0.0 collective-permute-done.3.refs_6_
  40.9 2.2 %collective-permute-done.2.refs_4_ = bf16[8,160,128]{2,1,0:T(8,128)(2,1)S(1)} collective-permute-done((bf16[8,160,128]{2,1,0:T(8,128)(2,1)S(1)}, bf16[8,160,128]{2,1,0:T(8,128)(2,1)S(1)}, u32[]{:S(2)}, u32[]{:S(2)}) %collective-permute-start.2) | collective-permute-done | bytes 327712 | tf_op jit(solution)/shard_map/ppermute | solution.py:226
  43.2 0.0 collective-permute-done.6.refs_2_.refs_10_
  43.2 0.0 collective-permute-start.8
  43.2 0.5 collective-permute-start.9
  43.7 0.0 collective-permute-start.10
  43.7 2.6 %collective-permute-start.13 = (bf16[8,96,128]{2,1,0:T(8,128)(2,1)S(1)}, bf16[8,96,128]{2,1,0:T(8,128)(2,1)S(1)}, u32[]{:S(2)}, u32[]{:S(2)}) collective-permute-start(bf16[8,96,128]{2,1,0:T(8,128)(2,1)S(1)} %get-tuple-element.69), channel_id=1, source_target_pairs={{6,0},{7,1},{4,2},{5,3},{2,4},{3,5},{0,6},{1,7},{14,8},{15,9},{12,... | collective-permute-start | bytes 589832 | tf_op jit(solution)/shard_map/ppermute | solution.py:226
  46.3 0.0 collective-permute-start.11
  46.3 0.0 collective-permute-done.9.refs_5_
  46.3 0.0 collective-permute-done.8.refs_3_.refs_11_
  46.3 1.7 %serve.2 = (bf16[8,160,128]{2,1,0:T(8,128)(2,1)S(1)}, bf16[8,160,128]{2,1,0:T(8,128)(2,1)S(1)}, bf16[8,160,128]{2,1,0:T(8,128)(2,1)S(1)}) custom-call(s32[4,16]{1,0:T(4,128)S(1)} %pad_add_fusion.asked, bf16[8,256,128]{2,1,0:T(8,128)(2,1)S(1)} %get-tuple-element.64.refs_0_.refs_8_, bf16[8,256,128]{2,1,0:T(8,128)(2,1)S(1)} %collective-permute-done.5.refs_1_.refs_9_, ...), custom_call_target="tpu_custom_call" | custom-call | flops 1000000000 | bytes 6000000 | tf_op jit(solution)/shard_map/serve/pallas_call | solution.py:291
  48.0 1.8 %collective-permute-start.15 = (bf16[8,160,128]{2,1,0:T(8,128)(2,1)S(1)}, bf16[8,160,128]{2,1,0:T(8,128)(2,1)S(1)}, u32[]{:S(2)}, u32[]{:S(2)}) collective-permute-start(bf16[8,160,128]{2,1,0:T(8,128)(2,1)S(1)} %get-tuple-element.70), channel_id=1, source_target_pairs={{8,0},{0,8},{24,16},{16,24},{9,1},{1,9},{25,17},{17,25},{10,2},{2,... | collective-permute-start | bytes 983048 | tf_op jit(solution)/shard_map/ppermute | solution.py:226
  49.8 1.2 %collective-permute-start.16 = (bf16[8,160,128]{2,1,0:T(8,128)(2,1)S(1)}, bf16[8,160,128]{2,1,0:T(8,128)(2,1)S(1)}, u32[]{:S(2)}, u32[]{:S(2)}) collective-permute-start(bf16[8,160,128]{2,1,0:T(8,128)(2,1)S(1)} %get-tuple-element.71), channel_id=1, source_target_pairs={{16,0},{24,8},{0,16},{8,24},{17,1},{25,9},{1,17},{9,25},{18,2},{26... | collective-permute-start | bytes 983048 | tf_op jit(solution)/shard_map/ppermute | solution.py:226
  51.0 0.6 collective-permute-start.17
  51.6 1.7 %collective-permute-done.13.refs_14_.refs_6_ = bf16[8,96,128]{2,1,0:T(8,128)(2,1)S(1)} collective-permute-done((bf16[8,96,128]{2,1,0:T(8,128)(2,1)S(1)}, bf16[8,96,128]{2,1,0:T(8,128)(2,1)S(1)}, u32[]{:S(2)}, u32[]{:S(2)}) %collective-permute-start.13) | collective-permute-done | bytes 196640 | tf_op jit(solution)/shard_map/ppermute | solution.py:226
  53.3 0.0 collective-permute-start.14
  53.3 9.6 %collective-permute-done.11.refs_12_.refs_4_ = bf16[8,96,128]{2,1,0:T(8,128)(2,1)S(1)} collective-permute-done((bf16[8,96,128]{2,1,0:T(8,128)(2,1)S(1)}, bf16[8,96,128]{2,1,0:T(8,128)(2,1)S(1)}, u32[]{:S(2)}, u32[]{:S(2)}) %collective-permute-start.11) | collective-permute-done | bytes 196640 | tf_op jit(solution)/shard_map/ppermute | solution.py:226
  62.9 0.0 collective-permute-start.12
  62.9 0.0 collective-permute-done.14.refs_15_.refs_7_
  62.9 1.4 %collective-permute-done.12.refs_13_.refs_5_ = bf16[8,96,128]{2,1,0:T(8,128)(2,1)S(1)} collective-permute-done((bf16[8,96,128]{2,1,0:T(8,128)(2,1)S(1)}, bf16[8,96,128]{2,1,0:T(8,128)(2,1)S(1)}, u32[]{:S(2)}, u32[]{:S(2)}) %collective-permute-start.12) | collective-permute-done | bytes 196640 | tf_op jit(solution)/shard_map/ppermute | solution.py:226
  64.3 0.0 collective-permute-done.15.refs_16_
  64.3 2.0 %collective-permute-done.16.refs_17_ = bf16[8,160,128]{2,1,0:T(8,128)(2,1)S(1)} collective-permute-done((bf16[8,160,128]{2,1,0:T(8,128)(2,1)S(1)}, bf16[8,160,128]{2,1,0:T(8,128)(2,1)S(1)}, u32[]{:S(2)}, u32[]{:S(2)}) %collective-permute-start.16) | collective-permute-done | bytes 327712 | tf_op jit(solution)/shard_map/ppermute | solution.py:226
  66.3 1.4 %serve.3 = (bf16[8,96,128]{2,1,0:T(8,128)(2,1)S(1)}, bf16[8,96,128]{2,1,0:T(8,128)(2,1)S(1)}, bf16[8,96,128]{2,1,0:T(8,128)(2,1)S(1)}) custom-call(s32[4,16]{1,0:T(4,128)S(1)} %pad_add_fusion.asked, bf16[8,256,128]{2,1,0:T(8,128)(2,1)S(1)} %get-tuple-element.64.refs_0_.refs_8_, bf16[8,256,128]{2,1,0:T(8,128)(2,1)S(1)} %collective-permute-done.5.refs_1_.refs_9_, ...), custom_call_target="tpu_custom_call" | custom-call | flops 1000000000 | bytes 6000000 | tf_op jit(solution)/shard_map/serve/pallas_call | solution.py:291
  67.8 1.2 %collective-permute-start.18 = (bf16[8,96,128]{2,1,0:T(8,128)(2,1)S(1)}, bf16[8,96,128]{2,1,0:T(8,128)(2,1)S(1)}, u32[]{:S(2)}, u32[]{:S(2)}) collective-permute-start(bf16[8,96,128]{2,1,0:T(8,128)(2,1)S(1)} %get-tuple-element.80), channel_id=1, source_target_pairs={{8,0},{0,8},{24,16},{16,24},{9,1},{1,9},{25,17},{17,25},{10,2},{2,... | collective-permute-start | bytes 589832 | tf_op jit(solution)/shard_map/ppermute | solution.py:226
  69.0 0.5 collective-permute-start.19
  69.5 1.8 %collective-permute-start.20 = (bf16[8,96,128]{2,1,0:T(8,128)(2,1)S(1)}, bf16[8,96,128]{2,1,0:T(8,128)(2,1)S(1)}, u32[]{:S(2)}, u32[]{:S(2)}) collective-permute-start(bf16[8,96,128]{2,1,0:T(8,128)(2,1)S(1)} %get-tuple-element.82), channel_id=1, source_target_pairs={{24,0},{16,8},{8,16},{0,24},{25,1},{17,9},{9,17},{1,25},{26,2},{18... | collective-permute-start | bytes 589832 | tf_op jit(solution)/shard_map/ppermute | solution.py:226
  71.3 0.0 copy-start.1
  71.3 2.2 %near.1 = bf16[16,128,192]{2,1,0:T(8,128)(2,1)S(1)} custom-call(s32[16]{0:T(128)S(1)} %copy-done.3, s32[16]{0:T(128)S(1)} %copy-done.2, bf16[8,256,128]{2,1,0:T(8,128)(2,1)S(1)} %get-tuple-element.64.refs_0_.refs_8_, bf16[8,256,128]{2,1,0:T(8,128)(2,1)S(1)} %collective-permute-done.5.refs_1_.refs_9_, ...), custom_call_target="tpu_custom_call" | custom-call | flops 1000000000 | bytes 10000000 | tf_op jit(solution)/shard_map/near/pallas_call | solution.py:329
  73.5 1.9 %collective-permute-done.18.refs_19_ = bf16[8,96,128]{2,1,0:T(8,128)(2,1)S(1)} collective-permute-done((bf16[8,96,128]{2,1,0:T(8,128)(2,1)S(1)}, bf16[8,96,128]{2,1,0:T(8,128)(2,1)S(1)}, u32[]{:S(2)}, u32[]{:S(2)}) %collective-permute-start.18) | collective-permute-done | bytes 196640 | tf_op jit(solution)/shard_map/ppermute | solution.py:226
  75.4 3.7 %collective-permute-done.19.refs_20_ = bf16[8,96,128]{2,1,0:T(8,128)(2,1)S(1)} collective-permute-done((bf16[8,96,128]{2,1,0:T(8,128)(2,1)S(1)}, bf16[8,96,128]{2,1,0:T(8,128)(2,1)S(1)}, u32[]{:S(2)}, u32[]{:S(2)}) %collective-permute-start.19) | collective-permute-done | bytes 196640 | tf_op jit(solution)/shard_map/ppermute | solution.py:226
  79.1 3.4 %far.1 = f32[16,128,128]{2,1,0:T(8,128)} custom-call(s32[16]{0:T(128)S(1)} %slice_bitcast_fusion.code, s32[16]{0:T(128)S(1)} %copy-done.2, bf16[16,128,192]{2,1,0:T(8,128)(2,1)S(1)} %near.1, bf16[8,256,128]{2,1,0:T(8,128)(2,1)S(1)} %get-tuple-element.64.refs_0_.refs_8_, bf16[8,256,128]{2,1,0:T(8,128)(2,1)S(1)} %collective-permute-done.5.refs_1_.refs_9_, ...), custom_call_target="tpu_custom_call" | custom-call | flops 1000000000 | bytes 13000000 | tf_op jit(solution)/shard_map/far/pallas_call | solution.py:387
  (21 shorter events, 0.1 us)
Async XLA Ops:
  0.6 14.9 %copy-start.4 = (f32[8,128,256]{2,1,0:T(8,128)S(1)}, f32[8,128,256]{2,1,0:T(8,128)}, u32[]{:S(2)}) copy-start(f32[8,128,256]{2,1,0:T(8,128)} %own_transfer.1) | copy-start | bytes 3145732
  0.6 7.6 %collective-permute-start.1 = (f32[8,128,256]{2,1,0:T(8,128)}, f32[8,128,256]{2,1,0:T(8,128)S(1)}, u32[]{:S(2)}, u32[]{:S(2)}) collective-permute-start(f32[8,128,256]{2,1,0:T(8,128)} %own_transfer.1), channel_id=1, source_target_pairs={{1,0},{0,1},{3,2},{2,3},{5,4},{4,5},{7,6},{6,7},{9,8},{8,9},{11,10... | collective-permute-start | bytes 3145736 | tf_op jit(solution)/shard_map/ppermute | solution.py:226
  1.2 7.1 %collective-permute-start = (bf16[8,256,128]{2,1,0:T(8,128)(2,1)}, bf16[8,256,128]{2,1,0:T(8,128)(2,1)S(1)}, u32[]{:S(2)}, u32[]{:S(2)}) collective-permute-start(bf16[8,256,128]{2,1,0:T(8,128)(2,1)} %own_basis.1), channel_id=1, source_target_pairs={{1,0},{0,1},{3,2},{2,3},{5,4},{4,5},{7,6},{6,7},{9,8},{8,9},{11,10... | collective-permute-start | bytes 1572872 | tf_op jit(solution)/shard_map/ppermute | solution.py:226
  1.2 1.0 %copy-start.5 = (bf16[8,256,128]{2,1,0:T(8,128)(2,1)S(1)}, bf16[8,256,128]{2,1,0:T(8,128)(2,1)}, u32[]{:S(2)}) copy-start(bf16[8,256,128]{2,1,0:T(8,128)(2,1)} %own_basis.1) | copy-start | bytes 1572868
  2.3 5.9 %copy-start.6 = (s32[16]{0:T(128)S(1)}, s32[16]{0:T(128)}, u32[]{:S(2)}) copy-start(s32[16]{0:T(128)} %param.15) | copy-start | bytes 196
  2.3 5.9 %copy-start.7 = (s32[16,1]{0,1:T(1,128)S(1)}, s32[16,1]{0,1:T(1,128)}, u32[]{:S(2)}) copy-start(s32[16,1]{0,1:T(1,128)} %param.14) | copy-start | bytes 196
  8.3 19.9 %collective-permute-start.5 = (bf16[8,256,128]{2,1,0:T(8,128)(2,1)S(1)}, bf16[8,256,128]{2,1,0:T(8,128)(2,1)S(1)}, u32[]{:S(2)}, u32[]{:S(2)}) collective-permute-start(bf16[8,256,128]{2,1,0:T(8,128)(2,1)S(1)} %get-tuple-element.64.refs_0_.refs_8_), channel_id=1, source_target_pairs={{1,0},{0,1},{3,2},{2,3},{5,4},{4,5},{7,6},{6,7},{9,8},{8,9},{11,10... | collective-permute-start | bytes 1572872 | tf_op jit(solution)/shard_map/ppermute | solution.py:226
  8.8 34.4 %collective-permute-start.6 = (bf16[8,256,128]{2,1,0:T(8,128)(2,1)S(1)}, bf16[8,256,128]{2,1,0:T(8,128)(2,1)S(1)}, u32[]{:S(2)}, u32[]{:S(2)}) collective-permute-start(bf16[8,256,128]{2,1,0:T(8,128)(2,1)S(1)} %get-tuple-element.64.refs_0_.refs_8_), channel_id=1, source_target_pairs={{2,0},{3,1},{0,2},{1,3},{6,4},{7,5},{4,6},{5,7},{10,8},{11,9},{8,1... | collective-permute-start | bytes 1572872 | tf_op jit(solution)/shard_map/ppermute | solution.py:226
  11.4 29.5 %collective-permute-start.3 = (bf16[8,160,128]{2,1,0:T(8,128)(2,1)S(1)}, bf16[8,160,128]{2,1,0:T(8,128)(2,1)S(1)}, u32[]{:S(2)}, u32[]{:S(2)}) collective-permute-start(bf16[8,160,128]{2,1,0:T(8,128)(2,1)S(1)} %get-tuple-element.46), channel_id=1, source_target_pairs={{6,0},{7,1},{4,2},{5,3},{2,4},{3,5},{0,6},{1,7},{14,8},{15,9},{12,... | collective-permute-start | bytes 983048 | tf_op jit(solution)/shard_map/ppermute | solution.py:226
  13.9 29.3 %collective-permute-start.2 = (bf16[8,160,128]{2,1,0:T(8,128)(2,1)S(1)}, bf16[8,160,128]{2,1,0:T(8,128)(2,1)S(1)}, u32[]{:S(2)}, u32[]{:S(2)}) collective-permute-start(bf16[8,160,128]{2,1,0:T(8,128)(2,1)S(1)} %get-tuple-element.46), channel_id=1, source_target_pairs={{4,0},{5,1},{6,2},{7,3},{0,4},{1,5},{2,6},{3,7},{12,8},{13,9},{14,... | collective-permute-start | bytes 983048 | tf_op jit(solution)/shard_map/ppermute | solution.py:226
  14.0 14.1 %collective-permute-start.4 = (s32[1,16]{1,0:T(1,128)S(1)}, s32[1,16]{1,0:T(1,128)S(1)}, u32[]{:S(2)}, u32[]{:S(2)}) collective-permute-start(s32[1,16]{1,0:T(1,128)S(1)} %bitcast.9), channel_id=1, source_target_pairs={{8,0},{0,8},{24,16},{16,24},{9,1},{1,9},{25,17},{17,25},{10,2},{2,... | collective-permute-start | bytes 200 | tf_op jit(solution)/shard_map/ppermute | solution.py:226
  28.2 12.7 %collective-permute-start.7 = (s32[2,16]{1,0:T(2,128)S(1)}, s32[2,16]{1,0:T(2,128)S(1)}, u32[]{:S(2)}, u32[]{:S(2)}) collective-permute-start(s32[2,16]{1,0:T(2,128)S(1)} %pad_add_fusion.1), channel_id=1, source_target_pairs={{16,0},{24,8},{0,16},{8,24},{17,1},{25,9},{1,17},{9,25},{18,2},{26... | collective-permute-start | bytes 392 | tf_op jit(solution)/shard_map/ppermute | solution.py:226
  43.2 3.2 %collective-permute-start.8 = (bf16[8,256,128]{2,1,0:T(8,128)(2,1)S(1)}, bf16[8,256,128]{2,1,0:T(8,128)(2,1)S(1)}, u32[]{:S(2)}, u32[]{:S(2)}) collective-permute-start(bf16[8,256,128]{2,1,0:T(8,128)(2,1)S(1)} %collective-permute-done.6.refs_2_.refs_10_), channel_id=1, source_target_pairs={{1,0},{0,1},{3,2},{2,3},{5,4},{4,5},{7,6},{6,7},{9,8},{8,9},{11,10... | collective-permute-start | bytes 1572872 | tf_op jit(solution)/shard_map/ppermute | solution.py:226
  43.2 3.2 %collective-permute-start.9 = (bf16[8,160,128]{2,1,0:T(8,128)(2,1)S(1)}, bf16[8,160,128]{2,1,0:T(8,128)(2,1)S(1)}, u32[]{:S(2)}, u32[]{:S(2)}) collective-permute-start(bf16[8,160,128]{2,1,0:T(8,128)(2,1)S(1)} %collective-permute-done.2.refs_4_), channel_id=1, source_target_pairs={{1,0},{0,1},{3,2},{2,3},{5,4},{4,5},{7,6},{6,7},{9,8},{8,9},{11,10... | collective-permute-start | bytes 983048 | tf_op jit(solution)/shard_map/ppermute | solution.py:226
  43.7 2.7 %collective-permute-start.10 = (bf16[8,160,128]{2,1,0:T(8,128)(2,1)S(1)}, bf16[8,160,128]{2,1,0:T(8,128)(2,1)S(1)}, u32[]{:S(2)}, u32[]{:S(2)}) collective-permute-start(bf16[8,160,128]{2,1,0:T(8,128)(2,1)S(1)} %collective-permute-done.3.refs_6_), channel_id=1, source_target_pairs={{1,0},{0,1},{3,2},{2,3},{5,4},{4,5},{7,6},{6,7},{9,8},{8,9},{11,10... | collective-permute-start | bytes 983048 | tf_op jit(solution)/shard_map/ppermute | solution.py:226
  43.7 9.6 %collective-permute-start.13 = (bf16[8,96,128]{2,1,0:T(8,128)(2,1)S(1)}, bf16[8,96,128]{2,1,0:T(8,128)(2,1)S(1)}, u32[]{:S(2)}, u32[]{:S(2)}) collective-permute-start(bf16[8,96,128]{2,1,0:T(8,128)(2,1)S(1)} %get-tuple-element.69), channel_id=1, source_target_pairs={{6,0},{7,1},{4,2},{5,3},{2,4},{3,5},{0,6},{1,7},{14,8},{15,9},{12,... | collective-permute-start | bytes 589832 | tf_op jit(solution)/shard_map/ppermute | solution.py:226
  46.3 16.6 %collective-permute-start.11 = (bf16[8,96,128]{2,1,0:T(8,128)(2,1)S(1)}, bf16[8,96,128]{2,1,0:T(8,128)(2,1)S(1)}, u32[]{:S(2)}, u32[]{:S(2)}) collective-permute-start(bf16[8,96,128]{2,1,0:T(8,128)(2,1)S(1)} %get-tuple-element.69), channel_id=1, source_target_pairs={{4,0},{5,1},{6,2},{7,3},{0,4},{1,5},{2,6},{3,7},{12,8},{13,9},{14,... | collective-permute-start | bytes 589832 | tf_op jit(solution)/shard_map/ppermute | solution.py:226
  48.0 16.3 %collective-permute-start.15 = (bf16[8,160,128]{2,1,0:T(8,128)(2,1)S(1)}, bf16[8,160,128]{2,1,0:T(8,128)(2,1)S(1)}, u32[]{:S(2)}, u32[]{:S(2)}) collective-permute-start(bf16[8,160,128]{2,1,0:T(8,128)(2,1)S(1)} %get-tuple-element.70), channel_id=1, source_target_pairs={{8,0},{0,8},{24,16},{16,24},{9,1},{1,9},{25,17},{17,25},{10,2},{2,... | collective-permute-start | bytes 983048 | tf_op jit(solution)/shard_map/ppermute | solution.py:226
  49.8 16.5 %collective-permute-start.16 = (bf16[8,160,128]{2,1,0:T(8,128)(2,1)S(1)}, bf16[8,160,128]{2,1,0:T(8,128)(2,1)S(1)}, u32[]{:S(2)}, u32[]{:S(2)}) collective-permute-start(bf16[8,160,128]{2,1,0:T(8,128)(2,1)S(1)} %get-tuple-element.71), channel_id=1, source_target_pairs={{16,0},{24,8},{0,16},{8,24},{17,1},{25,9},{1,17},{9,25},{18,2},{26... | collective-permute-start | bytes 983048 | tf_op jit(solution)/shard_map/ppermute | solution.py:226
  51.0 20.3 %copy-start = (bf16[16,256,192]{1,2,0:T(8,128)(2,1)S(1)}, bf16[16,256,192]{1,2,0:T(8,128)(2,1)}, u32[]{:S(2)}) copy-start(bf16[16,256,192]{1,2,0:T(8,128)(2,1)} %param.10) | copy-start | bytes 4718596
  51.0 20.3 %copy-start.2 = (s32[16]{0:T(128)S(1)}, s32[16]{0:T(128)}, u32[]{:S(2)}) copy-start(s32[16]{0:T(128)} %slabs.3) | copy-start | bytes 196
  51.0 20.3 %copy-start.3 = (s32[16]{0:T(128)S(1)}, s32[16]{0:T(128)}, u32[]{:S(2)}) copy-start(s32[16]{0:T(128)} %leaf.1) | copy-start | bytes 196
  51.0 15.3 %collective-permute-start.17 = (bf16[8,160,128]{2,1,0:T(8,128)(2,1)S(1)}, bf16[8,160,128]{2,1,0:T(8,128)(2,1)S(1)}, u32[]{:S(2)}, u32[]{:S(2)}) collective-permute-start(bf16[8,160,128]{2,1,0:T(8,128)(2,1)S(1)} %get-tuple-element.72), channel_id=1, source_target_pairs={{24,0},{16,8},{8,16},{0,24},{25,1},{17,9},{9,17},{1,25},{26,2},{18... | collective-permute-start | bytes 983048 | tf_op jit(solution)/shard_map/ppermute | solution.py:226
  53.3 9.6 %collective-permute-start.14 = (bf16[8,96,128]{2,1,0:T(8,128)(2,1)S(1)}, bf16[8,96,128]{2,1,0:T(8,128)(2,1)S(1)}, u32[]{:S(2)}, u32[]{:S(2)}) collective-permute-start(bf16[8,96,128]{2,1,0:T(8,128)(2,1)S(1)} %collective-permute-done.13.refs_14_.refs_6_), channel_id=1, source_target_pairs={{1,0},{0,1},{3,2},{2,3},{5,4},{4,5},{7,6},{6,7},{9,8},{8,9},{11,10... | collective-permute-start | bytes 589832 | tf_op jit(solution)/shard_map/ppermute | solution.py:226
  62.9 1.4 %collective-permute-start.12 = (bf16[8,96,128]{2,1,0:T(8,128)(2,1)S(1)}, bf16[8,96,128]{2,1,0:T(8,128)(2,1)S(1)}, u32[]{:S(2)}, u32[]{:S(2)}) collective-permute-start(bf16[8,96,128]{2,1,0:T(8,128)(2,1)S(1)} %collective-permute-done.11.refs_12_.refs_4_), channel_id=1, source_target_pairs={{1,0},{0,1},{3,2},{2,3},{5,4},{4,5},{7,6},{6,7},{9,8},{8,9},{11,10... | collective-permute-start | bytes 589832 | tf_op jit(solution)/shard_map/ppermute | solution.py:226
  67.8 7.6 %collective-permute-start.18 = (bf16[8,96,128]{2,1,0:T(8,128)(2,1)S(1)}, bf16[8,96,128]{2,1,0:T(8,128)(2,1)S(1)}, u32[]{:S(2)}, u32[]{:S(2)}) collective-permute-start(bf16[8,96,128]{2,1,0:T(8,128)(2,1)S(1)} %get-tuple-element.80), channel_id=1, source_target_pairs={{8,0},{0,8},{24,16},{16,24},{9,1},{1,9},{25,17},{17,25},{10,2},{2,... | collective-permute-start | bytes 589832 | tf_op jit(solution)/shard_map/ppermute | solution.py:226
  69.0 10.1 %collective-permute-start.19 = (bf16[8,96,128]{2,1,0:T(8,128)(2,1)S(1)}, bf16[8,96,128]{2,1,0:T(8,128)(2,1)S(1)}, u32[]{:S(2)}, u32[]{:S(2)}) collective-permute-start(bf16[8,96,128]{2,1,0:T(8,128)(2,1)S(1)} %get-tuple-element.81), channel_id=1, source_target_pairs={{16,0},{24,8},{0,16},{8,24},{17,1},{25,9},{1,17},{9,25},{18,2},{26... | collective-permute-start | bytes 589832 | tf_op jit(solution)/shard_map/ppermute | solution.py:226
  69.5 9.6 %collective-permute-start.20 = (bf16[8,96,128]{2,1,0:T(8,128)(2,1)S(1)}, bf16[8,96,128]{2,1,0:T(8,128)(2,1)S(1)}, u32[]{:S(2)}, u32[]{:S(2)}) collective-permute-start(bf16[8,96,128]{2,1,0:T(8,128)(2,1)S(1)} %get-tuple-element.82), channel_id=1, source_target_pairs={{24,0},{16,8},{8,16},{0,24},{25,1},{17,9},{9,17},{1,25},{26,2},{18... | collective-permute-start | bytes 589832 | tf_op jit(solution)/shard_map/ppermute | solution.py:226
  71.3 7.8 %copy-start.1 = (bf16[16,256,192]{1,2,0:T(8,128)(2,1)S(1)}, bf16[16,256,192]{1,2,0:T(8,128)(2,1)}, u32[]{:S(2)}) copy-start(bf16[16,256,192]{1,2,0:T(8,128)(2,1)} %param.11) | copy-start | bytes 4718596
